TPU v7x, 128 devices: a whole 4x4x4 slice. The times are simulated.
128 devices in a mesh: dp: 16 (over x, z_lo, core), pipe: 8 (over y, z_hi).
Axes of the slice: x: 4, y: 4, z: 4 (z_hi: 2, z_lo: 2; z = z_hi * 2 + z_lo), core: 2. Of those that a mesh axis runs over, the one named last changes fastest.
Arguments:
- shallow: bfloat16 [4096, 8192], P('dp'), may hold values from -8 to 8
- teacher: bfloat16 [4096, 8192], P(('dp', 'pipe')), may hold values from -8 to 8
- positions: int32 [4096], P('dp'), may hold values from 0 to 4095
- segments: int32 [4096], P('dp'), may hold values from 0 to 255, never falling along the last dimension, each value on 1 to 64 neighbouring positions
- in_gain: float32 [8192], replicated, may hold values from 0.2 to 4.5
- w_query: bfloat16 [8192, 4096], P('dp', 'pipe'), may hold values from -0.0625 to 0.0625
- w_keyval: bfloat16 [8192, 1024], P('dp', 'pipe'), may hold values from -0.0625 to 0.0625
- w_output: bfloat16 [4096, 8192], P('pipe', 'dp'), may hold values from -0.09375 to 0.09375
Outputs:
- loss: float32 [], replicated
- step_query: float32 [8192, 4096], P('dp', 'pipe')
- step_keyval: float32 [8192, 1024], P('dp', 'pipe')
- step_output: float32 [4096, 8192], P('pipe', 'dp')
Inputs may be any that keep to these rules, and one draw needn't show every extreme that they name: `segments`: ids never fall along the rows; every segment covers 1 to 64 rows.
All inputs are finite; a program needn't handle non-finite values.
Results may differ from a plain program's by a relative error of at most 0.023.
Values may be sent and summed in bfloat16 or wider, within the bound.
A program may use at most 128 MiB of HBM per device.

v0:
```python
import math

import jax
import jax.numpy as jnp
from jax import lax
from jax.sharding import PartitionSpec as P

D = 8192
HD = 128
QH = 32
KV = 4


theta_base = 10000.0
norm_eps = 1e-05
cosine_eps = 1e-06
mean_eps = 1e-12
mask_fill = -1e30


def shifted(value, axis, steps):
    count = lax.axis_size(axis)
    pairs = [(source, (source + steps) % count) for source in range(count)]
    return lax.ppermute(value, axis, pairs)


def normalize_rows(rows_in, in_gain):
    widened = rows_in.astype(jnp.float32)
    spread = jnp.mean(widened * widened, axis=-1, keepdims=True)
    return (widened * lax.rsqrt(spread + norm_eps) * in_gain[None, :]).astype(jnp.bfloat16)


def rotary_tables(positions, head_width):
    half_width = head_width // 2
    exponent = jnp.arange(half_width).astype(jnp.float32) * (2.0 / head_width)
    inverse = jnp.power(jnp.float32(theta_base), -exponent)
    angle_table = positions.astype(jnp.float32)[:, None] * inverse[None, :]
    return (jnp.cos(angle_table), jnp.sin(angle_table))


def rotate(values, cosine, sine_table):
    half_width = values.shape[-1] // 2
    leading = values[..., :half_width]
    trailing = values[..., half_width:]
    cosine_row = cosine[:, None, :]
    sine_row = sine_table[:, None, :]
    return jnp.concatenate(
        [leading * cosine_row - trailing * sine_row, trailing * cosine_row + leading * sine_row],
        axis=-1,
    )


def unrotate(values, cosine, sine_table):
    half_width = values.shape[-1] // 2
    leading = values[..., :half_width]
    trailing = values[..., half_width:]
    cosine_row = cosine[:, None, :]
    sine_row = sine_table[:, None, :]
    return jnp.concatenate(
        [leading * cosine_row + trailing * sine_row, trailing * cosine_row - leading * sine_row],
        axis=-1,
    )


def attend(queries, keys_head, values_head, allowed):
    score_scale = 1.0 / math.sqrt(queries.shape[-1])
    scores = (
        jnp.einsum("rhd,khd->hrk", queries, keys_head, preferred_element_type=jnp.float32)
        * score_scale
    )
    scores = jnp.where(allowed[None], scores, mask_fill)
    highest = jnp.max(scores, axis=-1, keepdims=True)
    weights = jnp.exp(scores - highest)
    softmax_rows = weights / jnp.sum(weights, axis=-1, keepdims=True)
    softmax_low = softmax_rows.astype(jnp.bfloat16)
    attended = jnp.einsum(
        "hrk,khd->rhd", softmax_low, values_head, preferred_element_type=jnp.float32
    ).astype(jnp.bfloat16)
    return (softmax_rows, softmax_low, attended)


def attend_grad(softmax_rows, softmax_low, queries, keys_head, values_head, att_grad):
    score_scale = 1.0 / math.sqrt(queries.shape[-1])
    inner_prod = jnp.einsum(
        "rhd,khd->hrk", att_grad, values_head, preferred_element_type=jnp.float32
    )
    centred = inner_prod - jnp.sum(softmax_rows * inner_prod, axis=-1, keepdims=True)
    score_grad = (softmax_rows * centred * score_scale).astype(jnp.bfloat16)
    query_part = jnp.einsum(
        "hrk,khd->rhd", score_grad, keys_head, preferred_element_type=jnp.float32
    )
    key_part = jnp.einsum("hrk,rhd->khd", score_grad, queries, preferred_element_type=jnp.float32)
    value_part = jnp.einsum(
        "hrk,rhd->khd", softmax_low, att_grad, preferred_element_type=jnp.float32
    )
    return (query_part, key_part, value_part)


def held_low(values):
    return lax.optimization_barrier(values.astype(jnp.bfloat16)).astype(jnp.float32)


def contract_rows(left, right):
    return lax.dot_general(
        left, right, (((0,), (0,)), ((), ())), preferred_element_type=jnp.float32
    )


def contract_cols(left, right):
    return lax.dot_general(
        left, right, (((1,), (1,)), ((), ())), preferred_element_type=jnp.float32
    )


def per_device(shallow, teacher, positions, segments, in_gain, w_query, w_keyval, w_output):
    group_rows = shallow.shape[0]
    pipe_count = lax.axis_size("pipe")
    data_count = lax.axis_size("dp")
    pipe_rank = lax.axis_index("pipe")
    block_rows = group_rows // pipe_count
    head_cols = w_query.shape[1]
    local_heads = head_cols // HD
    keyval_cols = w_keyval.shape[1]
    keyval_blocks = keyval_cols // HD
    all_rows = group_rows * data_count
    param_count = D * (2 * QH * HD + 2 * KV * HD)
    normed = normalize_rows(shallow, in_gain)
    cosine, sine_table = rotary_tables(positions, HD)
    columns = normed
    query_proj = jnp.dot(
        columns,
        lax.all_gather(w_query, "dp", axis=0, tiled=True),
        preferred_element_type=jnp.float32,
    )
    keyval_proj = jnp.dot(
        columns,
        lax.all_gather(w_keyval, "dp", axis=0, tiled=True),
        preferred_element_type=jnp.float32,
    )
    queries = rotate(query_proj.reshape(group_rows, local_heads, HD), cosine, sine_table).astype(
        jnp.bfloat16
    )
    keyval_local = keyval_proj.reshape(group_rows, keyval_blocks, HD)
    block_ids = pipe_rank * keyval_blocks + jnp.arange(keyval_blocks)
    is_key = (block_ids % 2 == 0)[None, :, None]
    keyval_local = jnp.where(is_key, rotate(keyval_local, cosine, sine_table), keyval_local).astype(
        jnp.bfloat16
    )
    keyval_all = lax.all_gather(
        keyval_local.reshape(group_rows, keyval_cols), "pipe", axis=1, tiled=True
    )
    keyval_all = keyval_all.reshape(group_rows, KV, 2, HD)
    head_ids = pipe_rank * local_heads + jnp.arange(local_heads)
    chooser = head_ids[:, None] % KV == jnp.arange(KV)[None, :]
    picked = jnp.einsum(
        "rksd,jk->rjsd",
        keyval_all,
        chooser.astype(jnp.bfloat16),
        preferred_element_type=jnp.float32,
    ).astype(jnp.bfloat16)
    keys_head = picked[:, :, 0]
    values_head = picked[:, :, 1]
    row_order = jnp.arange(group_rows)
    allowed = (segments[:, None] == segments[None, :]) & (row_order[None, :] <= row_order[:, None])
    softmax_rows, softmax_low, attended = attend(queries, keys_head, values_head, allowed)
    att_flat = attended.reshape(group_rows, head_cols)
    shallow_block = lax.dynamic_slice_in_dim(shallow, pipe_rank * block_rows, block_rows, 0)
    target = shifted(teacher, "pipe", 1).astype(jnp.float32)
    w_out_full = lax.all_gather(w_output, "dp", axis=1, tiled=True)
    partial_value = held_low(jnp.dot(att_flat, w_out_full, preferred_element_type=jnp.float32))
    out_rows = lax.psum_scatter(
        partial_value.astype(jnp.bfloat16), "pipe", scatter_dimension=0, tiled=True
    ).astype(jnp.float32)
    output = shallow_block.astype(jnp.float32) + out_rows
    norm_out = jnp.sqrt(jnp.sum(output * output, axis=-1, keepdims=True) + cosine_eps)
    norm_tar = jnp.sqrt(jnp.sum(target * target, axis=-1, keepdims=True) + cosine_eps)
    cosine_sim = jnp.sum(output * target, axis=-1, keepdims=True) / (norm_out * norm_tar)
    loss_local = jnp.sum(1.0 - cosine_sim)
    out_grad = (
        -(target / (norm_out * norm_tar) - cosine_sim * output / (norm_out * norm_out)) / all_rows
    ).astype(jnp.bfloat16)
    loss_total = lax.psum(loss_local, ("dp", "pipe"))
    grad_all = lax.all_gather(out_grad, "pipe", axis=0, tiled=True)
    att_grad = contract_cols(grad_all, w_out_full).astype(jnp.bfloat16)
    att_grad = att_grad.reshape(group_rows, local_heads, HD)
    query_part, key_part, value_part = attend_grad(
        softmax_rows, softmax_low, queries, keys_head, values_head, att_grad
    )
    query_grad = (
        unrotate(query_part, cosine, sine_table).astype(jnp.bfloat16).reshape(group_rows, head_cols)
    )
    spread_back = jnp.einsum(
        "rjsd,jk->rksd", jnp.stack([key_part, value_part], axis=2), chooser.astype(jnp.float32)
    )
    keyval_sum = lax.psum_scatter(
        spread_back.reshape(group_rows, 2 * KV * HD).astype(jnp.bfloat16),
        "pipe",
        scatter_dimension=1,
        tiled=True,
    ).astype(jnp.float32)
    keyval_sum = keyval_sum.reshape(group_rows, keyval_blocks, HD)
    keyval_grad = (
        jnp.where(is_key, unrotate(keyval_sum, cosine, sine_table), keyval_sum)
        .astype(jnp.bfloat16)
        .reshape(group_rows, keyval_cols)
    )
    grad_inputs = jnp.concatenate([query_grad, keyval_grad], axis=1)
    columns = normed
    grad_shard = lax.psum_scatter(
        jnp.concatenate(
            [contract_rows(columns, grad_inputs), contract_rows(grad_all, att_flat)], axis=1
        ).astype(jnp.bfloat16),
        "dp",
        scatter_dimension=0,
        tiled=True,
    ).astype(jnp.float32)
    grad_query = grad_shard[:, :head_cols]
    grad_keyval = grad_shard[:, head_cols : head_cols + keyval_cols]
    grad_output = grad_shard[:, head_cols + keyval_cols :].T
    squares = (
        jnp.sum(grad_query * grad_query)
        + jnp.sum(grad_keyval * grad_keyval)
        + jnp.sum(grad_output * grad_output)
    )
    square_total = lax.psum(squares, ("dp", "pipe"))
    grad_rms = jnp.sqrt(square_total / param_count + mean_eps)
    return (
        loss_total / all_rows,
        grad_query / grad_rms,
        grad_keyval / grad_rms,
        grad_output / grad_rms,
    )


def solution(mesh):
    placed = (
        P("dp", None),
        P(("dp", "pipe"), None),
        P("dp"),
        P("dp"),
        P(),
        P("dp", "pipe"),
        P("dp", "pipe"),
        P("pipe", "dp"),
    )
    return jax.shard_map(
        per_device,
        mesh=mesh,
        in_specs=placed,
        out_specs=(P(), P("dp", "pipe"), P("dp", "pipe"), P("pipe", "dp")),
        check_vma=False,
    )
```

profile of v0, /device:TPU:1, one launch (start us, length us, event | category | flops | bytes accessed | tf_op | source)
XLA Modules:
  0.0 725.1 jit_solution(165572289338817264)
XLA Ops:
  10.2 3.1 fusion.2
  14.7 32.7 %all-gather.5.cloned.1.call-done = bf16[8192,128]{1,0:T(8,128)(2,1)} async-done(((bf16[512,128]{1,0:T(8,128)(2,1)}), bf16[8192,128]{1,0:T(8,128)(2,1)}) %all-gather.5.cloned.1.call-update) | async-done | bytes 2097168 | tf_op jit(solution)/shard_map/all_gather | solution.py:137
  47.4 4.6 fusion.72
  52.4 29.5 %all_gather.16 = bf16[256,1024]{0,1:T(8,128)(2,1)S(1)} all-gather(bf16[256,128]{0,1:T(8,128)(2,1)S(1)} %fusion.37), channel_id=1, replica_groups=mesh['dp'=16,'pipe'=8] {'pipe'}, dimensions={1}, use_global_device_ids=true | all-gather | bytes 589824 | tf_op jit(solution)/shard_map/all_gather | solution.py:149
  83.0 26.8 %all-gather.7.cloned.1.call-done = bf16[8192,512]{1,0:T(8,128)(2,1)} async-done(((bf16[512,512]{1,0:T(8,128)(2,1)}), bf16[8192,512]{1,0:T(8,128)(2,1)}) %all-gather.7.cloned.1.call-update) | async-done | bytes 8388624 | tf_op jit(solution)/shard_map/all_gather | solution.py:132
  109.8 7.0 fusion.70
  118.4 45.1 %all-gather.9.cloned.1.call-done = bf16[512,8192]{1,0:T(8,128)(2,1)} async-done(((bf16[512,512]{1,0:T(8,128)(2,1)}), bf16[512,8192]{1,0:T(8,128)(2,1)}) %all-gather.9.cloned.1.call-update) | async-done | bytes 8388624 | tf_op jit(solution)/shard_map/all_gather | solution.py:169
  163.5 7.8 %convolution_convert_fusion.2 = bf16[256,8192]{1,0:T(8,128)(2,1)} fusion(bf16[256,512]{0,1:T(8,128)(2,1)S(1)} %bitcast.64, bf16[512,8192]{1,0:T(8,128)(2,1)} %all-gather.9.cloned.1.call-done), kind=kOutput, calls=%fused_computation.7 | convolution fusion | flops 2149580800 | bytes 12845056 | tf_op jit(solution)/shard_map/dot_general | solution.py:170
  171.4 2.9 collective-permute-start
  174.3 15.5 %collective-permute-done = bf16[32,8192]{1,0:T(8,128)(2,1)S(1)} collective-permute-done((bf16[32,8192]{1,0:T(8,128)(2,1)S(1)}, bf16[32,8192]{1,0:T(8,128)(2,1)S(1)}, u32[]{:S(2)}, u32[]{:S(2)}) %collective-permute-start) | collective-permute-done | bytes 524320 | tf_op jit(solution)/shard_map/ppermute | solution.py:24
  189.8 69.8 %reduce-scatter.4.cloned.1.call-done = bf16[32,8192]{1,0:T(8,128)(2,1)} async-done(((bf16[256,8192]{1,0:T(8,128)(2,1)}), bf16[32,8192]{1,0:T(8,128)(2,1)}) %reduce-scatter.4.cloned.1.call-update) | async-done | bytes 524304 | tf_op jit(solution)/shard_map/reduce_scatter | solution.py:171
  259.6 1.7 multiply_reduce_fusion.2
  261.9 2.4 fusion.19
  264.4 71.0 %all-gather.11.cloned.1.call-done = bf16[256,8192]{1,0:T(8,128)(2,1)} async-done(((bf16[32,8192]{1,0:T(8,128)(2,1)}), bf16[256,8192]{1,0:T(8,128)(2,1)}) %all-gather.11.cloned.1.call-update) | async-done | bytes 4194320 | tf_op jit(solution)/shard_map/all_gather | solution.py:183
  335.3 7.0 convolution_convert_fusion.6
  343.1 2.1 convolution_bitcast_fusion.1
  345.3 2.1 convolution_bitcast_fusion.2
  349.9 7.9 %convolution_convert_fusion.1 = bf16[8192,512]{0,1:T(8,128)(2,1)} fusion(bf16[256,512]{0,1:T(8,128)(2,1)S(1)} %bitcast.65, bf16[256,8192]{1,0:T(8,128)(2,1)} %all-gather.11.cloned.1.call-done), kind=kOutput, calls=%fused_computation.4 | convolution fusion | flops 2151677952 | bytes 12845056 | tf_op jit(solution)/shard_map/dot_general | solution.py:104
  357.8 58.6 %reduce-scatter.6.cloned.1.call-done = bf16[256,128]{0,1:T(8,128)(2,1)} async-done(((bf16[256,1024]{0,1:T(8,128)(2,1)}), bf16[256,128]{0,1:T(8,128)(2,1)}) %reduce-scatter.6.cloned.1.call-update) | async-done | bytes 65552 | tf_op jit(solution)/shard_map/reduce_scatter | solution.py:195
  418.5 5.8 convolution_convert_fusion
  424.3 13.8 %pad_maximum_fusion = bf16[8192,1152]{0,1:T(8,128)(2,1)} fusion(bf16[8192,512]{0,1:T(8,128)(2,1)} %convolution_convert_fusion.1, bf16[8192,640]{0,1:T(8,128)(2,1)S(1)} %convolution_convert_fusion), kind=kLoop, calls=%fused_computation.2 | loop fusion | flops 37748736 | bytes 37748736 | tf_op jit(solution)/shard_map/concatenate | solution.py:210
  438.1 203.0 %reduce-scatter.8.cloned.1.call-done = bf16[512,1152]{0,1:T(8,128)(2,1)} async-done(((bf16[8192,1152]{0,1:T(8,128)(2,1)}), bf16[512,1152]{0,1:T(8,128)(2,1)}) %reduce-scatter.8.cloned.1.call-update) | async-done | bytes 1179664 | tf_op jit(solution)/shard_map/reduce_scatter | solution.py:209
  646.2 64.6 %all-reduce = (f32[]{:T(128)}, f32[]{:T(128)}) all-reduce(f32[]{:T(128)} %get-tuple-element.19, f32[]{:T(128)S(6)} %add.123), channel_id=1, replica_groups=mesh['dp'=16,'pipe'=8] {'dp','pipe'}, use_global_device_ids=true, to_apply=%region_8.9 | all-reduce | flops 2 | bytes 16 | tf_op jit(solution)/shard_map/psum | solution.py:182
  713.4 1.8 copy.53
  (59 shorter events, 19.8 us)
Async XLA Ops:
  7.2 40.2 %all-gather.5.cloned.1.call-start = ((), (), s32[]{:S(2)}) async-start(), calls=%async_computation.3 | async-start | bytes 2228224 | tf_op jit(solution)/shard_map/all_gather | solution.py:137
  7.9 101.9 %all-gather.7.cloned.1.call-start = ((), (), s32[]{:S(2)}) async-start(), calls=%async_computation.4 | async-start | bytes 8912896 | tf_op jit(solution)/shard_map/all_gather | solution.py:132
  8.6 154.9 %all-gather.9.cloned.1.call-start = ((), (), s32[]{:S(2)}) async-start(), calls=%async_computation.5 | async-start | bytes 8912896 | tf_op jit(solution)/shard_map/all_gather | solution.py:169
  9.4 250.3 %reduce-scatter.4.cloned.1.call-start = ((), (), s32[]{:S(2)}) async-start(), calls=%async_computation.6 | async-start | bytes 4718592 | tf_op jit(solution)/shard_map/reduce_scatter | solution.py:171
  10.1 99.7 %copy-start = (f32[8192]{0:T(1024)S(1)}, f32[8192]{0:T(1024)}, u32[]{:S(2)}) copy-start(f32[8192]{0:T(1024)} %param.12) | copy-start | bytes 98308
  118.1 45.4 %copy-start.2 = (f32[4,256,256]{1,2,0:T(8,128)}, f32[4,256,256]{1,2,0:T(8,128)S(1)}, u32[]{:S(2)}) copy-start(f32[4,256,256]{1,2,0:T(8,128)S(1)} %get-tuple-element.40) | copy-start | bytes 3145732
  163.5 7.9 %copy-start.1 = (bf16[32,8192]{1,0:T(8,128)(2,1)S(1)}, bf16[32,8192]{1,0:T(8,128)(2,1)}, u32[]{:S(2)}) copy-start(bf16[32,8192]{1,0:T(8,128)(2,1)} %param.9) | copy-start | bytes 1572868
  171.3 164.0 %all-gather.11.cloned.1.call-start = ((), (), s32[]{:S(2)}) async-start(), calls=%async_computation.7 | async-start | bytes 4718592 | tf_op jit(solution)/shard_map/all_gather | solution.py:183
  171.4 18.4 %collective-permute-start = (bf16[32,8192]{1,0:T(8,128)(2,1)S(1)}, bf16[32,8192]{1,0:T(8,128)(2,1)S(1)}, u32[]{:S(2)}, u32[]{:S(2)}) collective-permute-start(bf16[32,8192]{1,0:T(8,128)(2,1)S(1)} %copy-done.1), channel_id=1, source_target_pairs={{0,1},{1,2},{2,3},{3,4},{4,5},{5,6},{6,7},{7,0},{8,9},{9,10},{10,1... | collective-permute-start | bytes 1572872 | tf_op jit(solution)/shard_map/ppermute | solution.py:24
  264.3 78.2 %copy-start.3 = (f32[4,256,256]{1,2,0:T(8,128)S(1)}, f32[4,256,256]{1,2,0:T(8,128)}, u32[]{:S(2)}) copy-start(f32[4,256,256]{1,2,0:T(8,128)} %copy-done.2) | copy-start | bytes 3145732
  264.3 152.1 %reduce-scatter.6.cloned.1.call-start = ((), (), s32[]{:S(2)}) async-start(), calls=%async_computation.8 | async-start | bytes 589824 | tf_op jit(solution)/shard_map/reduce_scatter | solution.py:195
  349.3 291.8 %reduce-scatter.8.cloned.1.call-start = ((), (), s32[]{:S(2)}) async-start(), calls=%async_computation.9 | async-start | bytes 20054016 | tf_op jit(solution)/shard_map/reduce_scatter | solution.py:209
Sparse Core Ops, SparseCore 0:
  9.7 37.6 all-gather.4
  49.1 60.6 all-gather.6
  111.5 51.9 all-gather.8
  171.4 88.1 reduce-scatter.3
  264.4 70.8 all-gather.10
  349.4 66.9 reduce-scatter.5
  438.2 202.8 reduce-scatter.7
where the time goes:
time: 726 us; the launch traced here: 725 us
  waiting for transfers between devices  525 us (72%)
  blocking collectives  94 us (13%)
  matrix products  46.8 us (6%)
  other arithmetic  31.7 us (4%)
  between operations  18.8 us (3%)
    reduce_scatter x1, waiting for transfers between devices, per_device(): lax.psum_scatter(jnp.concatenate([contract_rows(columns, grad_inputs), co...  203 us
    all_gather x1, waiting for transfers between devices, per_device(): grad_all = lax.all_gather(out_grad, 'pipe', axis=0, tiled=True)  71 us
    reduce_scatter x1, waiting for transfers between devices, per_device(): lax.psum_scatter(partial_value.astype(jnp.bfloat16), 'pipe', scatter_dime...  69.8 us
    psum x1, blocking collectives, per_device(): loss_total = lax.psum(loss_local, ('dp', 'pipe'))  64.6 us
    reduce_scatter x1, waiting for transfers between devices, per_device(): lax.psum_scatter(spread_back.reshape(group_rows, 2 * KV * HD).astype(jnp....  58.6 us
    all_gather x1, waiting for transfers between devices, per_device(): w_out_full = lax.all_gather(w_output, 'dp', axis=1, tiled=True)  45.1 us
    all_gather x1, waiting for transfers between devices, per_device(): lax.all_gather(w_keyval, 'dp', axis=0, tiled=True)  32.7 us
    all_gather x1, blocking collectives, per_device(): lax.all_gather(keyval_local.reshape(group_rows, keyval_cols), 'pipe', axi...  29.5 us
  transfers between devices with their start and end apart: 8, of which 8 were waited for; matrix products, arithmetic and copies ran while one was open for 4% of the time, Pallas kernels for 0%

commit v1 on v0

v1 whole, which is shorter than its diff:
```python
import functools
import math

import jax
import jax.numpy as jnp
from jax import lax
from jax.experimental import pallas as pl
from jax.experimental.pallas import tpu as pltpu
from jax.sharding import PartitionSpec as P

D = 8192
HD = 128
QH = 32
KV = 4
NP = 8
NX = 4
BLK = 512
ROWS = 256
HALF = 256
QUART = 128
WQ = 640

theta_base = 10000.0
norm_eps = 1e-05
cosine_eps = 1e-06
mean_eps = 1e-12
mask_fill = -1e30

MESH = pl.DeviceIdType.MESH
F32 = jnp.float32
BF16 = jnp.bfloat16
VLIM = 60 * 1024 * 1024


def remote(src, dst, send_sem, recv_sem, device):
    return pltpu.make_async_remote_copy(
        src_ref=src, dst_ref=dst, send_sem=send_sem, recv_sem=recv_sem,
        device_id=device, device_id_type=MESH,
    )


class Place:
    def __init__(self):
        dp = lax.axis_index("dp")
        self.dp = dp
        self.pipe = lax.axis_index("pipe")
        self.x = dp // 4
        self.z = (dp // 2) % 2
        self.c = dp % 2
        self.o = 1 - self.c
        self.slot = dp // 2
        self.swap_dp = self.pipe * 2 + self.c
        self.swap_pipe = self.slot
        self.swaps = self.slot != self.pipe

    def plane(self, dx, flip):
        z = 1 - self.z if flip else self.z
        return ((self.x + dx) % NX * 4 + z * 2 + self.c, self.pipe)

    def slot_of(self, dx, flip):
        z = 1 - self.z if flip else self.z
        return (self.x + dx) % NX * 2 + z

    def column(self, dj, other):
        dp = self.slot * 2 + (self.o if other else self.c)
        return (dp, (self.pipe + dj) % NP)

    def swap(self):
        return (self.swap_dp, self.swap_pipe)


def greet(devices, swap_place=None):
    barrier = pltpu.get_barrier_semaphore()
    for device in devices:
        pl.semaphore_signal(barrier, inc=1, device_id=device, device_id_type=MESH)
    if swap_place is None:
        pl.semaphore_wait(barrier, len(devices))
    else:
        @pl.when(swap_place.swaps)
        def _():
            pl.semaphore_signal(
                barrier, inc=1, device_id=swap_place.swap(), device_id_type=MESH
            )

        pl.semaphore_wait(barrier, len(devices) + swap_place.swaps.astype(jnp.int32))


GATHER = {
    "a_z": (0, 0, 0, HALF, "z"),
    "a_xp": (0, 0, 0, HALF, "p"),
    "a_xm": (0, 0, 0, HALF, "m"),
    "a_fp": (-1, 0, 0, QUART, "p"),
    "a_fm": (1, 0, QUART, QUART, "m"),
    "az_xp": (0, 1, 0, HALF, "p"),
    "az_xm": (0, 1, 0, HALF, "m"),
    "az_fp": (-1, 1, 0, QUART, "p"),
    "az_fm": (1, 1, QUART, QUART, "m"),
    "b_xp": (0, 0, HALF, HALF, "p"),
    "b_xm": (0, 0, HALF, HALF, "m"),
    "b_fp": (-1, 0, HALF, QUART, "p"),
    "b_fm": (1, 0, HALF + QUART, QUART, "m"),
    "b_z0": (0, 0, HALF, HALF, "z"),
    "b_zm": (-1, 0, HALF, HALF, "z"),
    "b_zp": (1, 0, HALF, HALF, "z"),
    "b_z2a": (2, 0, HALF, QUART, "z"),
    "b_z2b": (2, 0, HALF + QUART, QUART, "z"),
}
N_GATHER = len(GATHER)


class Gather:
    def __init__(self, place, buf, send_sems, recv_sems):
        self.place, self.buf = place, buf
        self.send_sems, self.recv_sems = send_sems, recv_sems
        self.order = {name: k for k, name in enumerate(GATHER)}

    def out(self, name):
        dx, flip, row, rows, way = GATHER[name]
        place = self.place
        k = self.order[name]
        region = self.buf.at[place.slot_of(dx, flip), pl.ds(row, rows)]
        device = {
            "p": place.plane(1, 0), "m": place.plane(-1, 0), "z": place.plane(0, 1)
        }[way]
        return remote(region, region, self.send_sems.at[k], self.recv_sems.at[k], device)

    def arrival(self, name):
        dx, flip, row, rows, way = GATHER[name]
        place = self.place
        k = self.order[name]
        dx = dx + {"p": -1, "m": 1, "z": 0}[way]
        flip = 1 - flip if way == "z" else flip
        region = self.buf.at[place.slot_of(dx, flip), pl.ds(row, rows)]
        return remote(
            region, region, self.send_sems.at[k], self.recv_sems.at[k], place.plane(0, 1)
        )

    def start(self, *names):
        for name in names:
            self.out(name).start()

    def wait(self, *names):
        for name in names:
            self.arrival(name).wait_recv()

    def begin(self):
        self.start("a_z", "a_xp", "a_xm", "b_xp", "b_xm", "b_z0")

    def middle(self):
        self.wait("a_z")
        self.start("az_xp", "az_xm")
        self.wait("a_xp")
        self.start("a_fp")
        self.wait("a_xm")
        self.start("a_fm")
        self.wait("b_xp")
        self.start("b_fp", "b_zm")
        self.wait("b_xm")
        self.start("b_fm", "b_zp")

    def late(self):
        self.wait("az_xp")
        self.start("az_fp")
        self.wait("az_xm")
        self.start("az_fm")
        self.wait("b_fp")
        self.start("b_z2a")
        self.wait("b_fm")
        self.start("b_z2b")

    def finish(self):
        self.wait("a_fp", "a_fm", "az_fp", "az_fm", "b_z0", "b_zm", "b_zp", "b_z2a", "b_z2b")

    def drain(self):
        for name in GATHER:
            self.out(name).wait_send()


def turned(v, cosine, sine):
    half = HD // 2
    rolled = jnp.concatenate([v[:, half:], v[:, :half]], axis=1)
    return v * cosine + rolled * sine


def front_kernel(
    shallow, gain, wq, wkv, wo, teacher, cosine, sine,
    q_out, kv_out, normed_out, wo_out, target_out,
    wbuf, nbuf, pbuf, acc, mine, theirs,
    w_send, w_recv, o_send, o_recv, n_send, n_recv, t_send, t_recv, k_send, k_recv,
    s_send, s_recv, local_sems,
):
    at = Place()
    column = [(dj, other) for other in (0, 1) for dj in range(NP) if (dj, other) != (0, 0)]
    greet(
        [at.plane(1, 0), at.plane(-1, 0), at.plane(0, 1)] + [at.column(*d) for d in column],
        at,
    )
    peer = at.column(0, 1)

    wbuf[at.slot, :, pl.ds(0, BLK)] = wq[...]
    wbuf[at.slot, :, pl.ds(BLK, HD)] = wkv[...]
    wg = Gather(at, wbuf, w_send, w_recv)
    og = Gather(at, wo_out, o_send, o_recv)
    wg.begin()

    swap = remote(wo, wo_out.at[at.pipe], s_send.at[0], s_recv.at[0], at.swap())
    keep = pltpu.make_async_copy(wo, wo_out.at[at.pipe], local_sems.at[0])

    @pl.when(at.swaps)
    def _():
        swap.start()

    @pl.when(jnp.logical_not(at.swaps))
    def _():
        keep.start()

    def target_copy(k):
        dj, other = column[k]
        core = at.o if other else at.c
        first = pl.multiple_of((((at.pipe + dj) % NP) * 2 + core) * BLK, BLK)
        return remote(
            teacher.at[:, pl.ds(first, BLK)],
            target_out.at[at.c, (at.pipe + 1) % NP],
            t_send.at[k], t_recv.at[k], at.column(dj, other),
        )

    def target_arrival(k):
        dj, other = column[k]
        core = at.o if other else at.c
        region = target_out.at[core, (at.pipe - dj + NP + 1) % NP]
        return remote(region, region, t_send.at[k], t_recv.at[k], peer)

    for k in range(len(column)):
        target_copy(k).start()
    first = pl.multiple_of((at.pipe * 2 + at.c) * BLK, BLK)
    own_target = pltpu.make_async_copy(
        teacher.at[:, pl.ds(first, BLK)], target_out.at[at.c, (at.pipe + 1) % NP], local_sems.at[1]
    )
    own_target.start()

    mine_rows = pl.multiple_of(at.c * ROWS, ROWS)
    their_rows = pl.multiple_of(at.o * ROWS, ROWS)

    @pl.loop(0, ROWS // 32)
    def _(step):
        rows = pl.ds(pl.multiple_of(step * 32, 32), 32)

        def squares(k, total):
            part = shallow[rows, pl.ds(pl.multiple_of(k * 1024, 1024), 1024)].astype(F32)
            return total + jnp.sum(part * part, axis=1, keepdims=True)

        total = lax.fori_loop(0, 8, squares, jnp.zeros((32, 1), F32))
        scale = lax.rsqrt(total / D + norm_eps)

        @pl.loop(0, NP)
        def _(k):
            here = pl.ds(pl.multiple_of((k * 2 + at.c) * BLK, BLK), BLK)
            there = pl.ds(pl.multiple_of((k * 2 + at.o) * BLK, BLK), BLK)
            nrows = pl.ds(pl.multiple_of(mine_rows + step * 32, 32), 32)
            nbuf[k, nrows, :] = (shallow[rows, here].astype(F32) * scale * gain[:, here]).astype(BF16)
            pbuf[k, rows, :] = (shallow[rows, there].astype(F32) * scale * gain[:, there]).astype(BF16)

    swapped_rows = nbuf.at[:, pl.ds(mine_rows, ROWS)]
    normed_copy = remote(pbuf, swapped_rows, n_send.at[0], n_recv.at[0], peer)
    normed_copy.start()

    wg.middle()
    landed = nbuf.at[:, pl.ds(their_rows, ROWS)]
    remote(pbuf, landed, n_send.at[0], n_recv.at[0], peer).wait_recv()
    save = pltpu.make_async_copy(nbuf, normed_out, local_sems.at[2])
    save.start()
    wg.late()

    @pl.when(at.swaps)
    def _():
        remote(wo, wo_out.at[at.slot], s_send.at[0], s_recv.at[0], at.swap()).wait_recv()
        swap.wait_send()

    @pl.when(jnp.logical_not(at.swaps))
    def _():
        keep.wait()

    og.begin()
    wg.finish()

    acc[...] = jnp.zeros_like(acc)

    @pl.loop(0, NP)
    def _(k):
        acc[...] += jnp.dot(nbuf[k], wbuf[k], preferred_element_type=F32)

    mine[...] = acc[pl.ds(their_rows, ROWS), :]
    sums = remote(mine, theirs, n_send.at[1], n_recv.at[1], peer)
    sums.start()
    og.middle()
    sums.wait_recv()

    cos_table, sin_table = cosine[...], sine[...]
    for head in range(BLK // HD):
        cols = pl.ds(head * HD, HD)
        v = acc[pl.ds(mine_rows, ROWS), cols] + theirs[:, cols]
        q_out[:, cols] = turned(v, cos_table, sin_table).astype(BF16)
    cols = pl.ds(BLK, HD)
    v = acc[pl.ds(mine_rows, ROWS), cols] + theirs[:, cols]
    is_key = (at.pipe % 2 == 0).astype(F32)
    kv_out[at.pipe] = (turned(v, cos_table, sin_table) * is_key + v * (1.0 - is_key)).astype(BF16)

    def kv_copy(dj):
        region = kv_out.at[at.pipe]
        return remote(region, region, k_send.at[dj], k_recv.at[dj], at.column(dj, 0))

    def kv_arrival(dj):
        region = kv_out.at[(at.pipe - dj + NP) % NP]
        return remote(region, region, k_send.at[dj], k_recv.at[dj], peer)

    for dj in range(1, NP):
        kv_copy(dj).start()
    og.late()
    og.finish()
    for dj in range(1, NP):
        kv_arrival(dj).wait_recv()
    for k in range(len(column)):
        target_arrival(k).wait_recv()

    own_target.wait()
    save.wait()
    normed_copy.wait_send()
    sums.wait_send()
    wg.drain()
    og.drain()
    for dj in range(1, NP):
        kv_copy(dj).wait_send()
    for k in range(len(column)):
        target_copy(k).wait_send()


def front(shallow, gain, wq, wkv, wo, teacher, cosine, sine):
    vmem = pl.BlockSpec(memory_space=pltpu.VMEM)
    anyspace = pl.BlockSpec(memory_space=pl.ANY)
    dma = pltpu.SemaphoreType.DMA
    return pl.pallas_call(
        front_kernel,
        out_shape=(
            jax.ShapeDtypeStruct((ROWS, BLK), BF16),
            jax.ShapeDtypeStruct((NP, ROWS, HD), BF16),
            jax.ShapeDtypeStruct((NP, 2 * ROWS, BLK), BF16),
            jax.ShapeDtypeStruct((NP, BLK, BLK), BF16),
            jax.ShapeDtypeStruct((2, NP, ROWS // NP, BLK), BF16),
        ),
        in_specs=[vmem, vmem, vmem, vmem, anyspace, anyspace, vmem, vmem],
        out_specs=(vmem, vmem, anyspace, anyspace, anyspace),
        scratch_shapes=[
            pltpu.VMEM((NP, BLK, WQ), BF16),
            pltpu.VMEM((NP, 2 * ROWS, BLK), BF16),
            pltpu.VMEM((NP, ROWS, BLK), BF16),
            pltpu.VMEM((2 * ROWS, WQ), F32),
            pltpu.VMEM((ROWS, WQ), F32),
            pltpu.VMEM((ROWS, WQ), F32),
            dma((N_GATHER,)), dma((N_GATHER,)), dma((N_GATHER,)), dma((N_GATHER,)),
            dma((2,)), dma((2,)), dma((15,)), dma((15,)), dma((NP,)), dma((NP,)),
            dma((1,)), dma((1,)), dma((3,)),
        ],
        compiler_params=pltpu.CompilerParams(
            collective_id=0, has_side_effects=True, vmem_limit_bytes=VLIM
        ),
        name="front",
    )(shallow, gain, wq, wkv, wo, teacher, cosine, sine)


COLUMN = [(dj, other) for other in (0, 1) for dj in range(NP) if (dj, other) != (0, 0)]


def nt(left, right):
    return lax.dot_general(
        left, right, (((1,), (1,)), ((), ())), preferred_element_type=F32
    )


def middle_kernel(
    attended, wo, shallow, target,
    grad_out, all_out, og_out, loss_out,
    abuf, wbuf, sbuf, acc, lanes, square, stat_send, stat_recv,
    part_mine, part_send, part_recv, sum_send, sum_recv,
    a_send, a_recv, f_send, f_recv, s_send, s_recv, p_send, p_recv, r_send, r_recv,
    h_send, h_recv, local_sems,
):
    at = Place()
    greet([at.column(*d) for d in COLUMN])
    peer = at.column(0, 1)
    mine_rows = pl.multiple_of(at.c * ROWS, ROWS)
    their_rows = pl.multiple_of(at.o * ROWS, ROWS)
    mine = pl.ds(mine_rows, ROWS)
    theirs = pl.ds(their_rows, ROWS)

    load = pltpu.make_async_copy(wo, wbuf, local_sems.at[0])
    load.start()
    abuf[at.pipe, mine, :] = attended[...]

    def share(dj):
        region = abuf.at[at.pipe, mine]
        return remote(region, region, a_send.at[dj], a_recv.at[dj], at.column(dj, 0))

    def arrival(dj):
        region = abuf.at[(at.pipe - dj + NP) % NP, mine]
        return remote(region, region, a_send.at[dj], a_recv.at[dj], peer)

    def forward(dj):
        region = abuf.at[(at.pipe - dj + NP) % NP, mine]
        return remote(region, region, f_send.at[dj], f_recv.at[dj], peer)

    def forwarded(dj):
        region = abuf.at[(at.pipe - dj + NP) % NP, theirs]
        return remote(region, region, f_send.at[dj], f_recv.at[dj], peer)

    for dj in range(1, NP):
        share(dj).start()
    forward(0).start()

    here = pl.ds(pl.multiple_of((at.pipe * 2 + at.c) * BLK, BLK), BLK)
    there = pl.ds(pl.multiple_of((at.pipe * 2 + at.o) * BLK, BLK), BLK)
    own_rows = pltpu.make_async_copy(shallow.at[:, here], sbuf.at[mine], local_sems.at[1])
    own_rows.start()
    peer_rows = remote(shallow.at[:, there], sbuf.at[mine], h_send.at[0], h_recv.at[0], peer)
    peer_rows.start()

    acc[...] = jnp.zeros_like(acc)
    load.wait()

    def multiply(dj):
        forwarded(dj).wait_recv()
        source = (at.pipe - dj + NP) % NP
        acc[...] += jnp.dot(abuf[source], wbuf[source], preferred_element_type=F32)

    for dj in range(1, NP):
        arrival(dj).wait_recv()
        forward(dj).start()
        multiply(dj - 1)
    multiply(NP - 1)
    save = pltpu.make_async_copy(abuf, all_out, local_sems.at[2])
    save.start()
    own_rows.wait()
    landed = sbuf.at[theirs]
    remote(landed, landed, h_send.at[0], h_recv.at[0], peer).wait_recv()

    lane = lax.broadcasted_iota(jnp.int32, (64, 128), 1)

    @pl.loop(0, 2 * ROWS // 64)
    def _(step):
        rows = pl.ds(pl.multiple_of(step * 64, 64), 64)
        output = acc[rows, :] + sbuf[rows, :].astype(F32)
        acc[rows, :] = output
        wanted = target[rows, :].astype(F32)
        oo = jnp.sum(output * output, axis=1, keepdims=True)
        tt = jnp.sum(wanted * wanted, axis=1, keepdims=True)
        ot = jnp.sum(output * wanted, axis=1, keepdims=True)
        lanes[rows, :] = jnp.where(lane == 0, oo, jnp.where(lane == 1, tt, jnp.where(lane == 2, ot, 0.0)))

    square[...] = lanes[...].T
    stat_send[...] = square[pl.ds(0, 8), :]

    def stat(k):
        return remote(stat_send, stat_recv.at[k], s_send.at[k], s_recv.at[k], at.column(*COLUMN[k]))

    for k in range(len(COLUMN)):
        stat(k).start()
    total = stat_send[...]
    for k in range(len(COLUMN)):
        stat(k).wait_recv()
    for k in range(len(COLUMN)):
        total = total + stat_recv[k]
    square[pl.ds(0, 8), :] = total
    lanes[...] = square[...].T

    def gradient(step, lost):
        rows = pl.ds(pl.multiple_of(step * 64, 64), 64)
        output = acc[rows, :]
        wanted = target[rows, :].astype(F32)
        norm_out = jnp.sqrt(lanes[rows, 0:1] + cosine_eps)
        norm_tar = jnp.sqrt(lanes[rows, 1:2] + cosine_eps)
        both = norm_out * norm_tar
        cosine = lanes[rows, 2:3] / both
        og = -(wanted * (1.0 / both) - output * (cosine / (norm_out * norm_out))) * (1.0 / 4096)
        og_out[rows, :] = og.astype(BF16)
        return lost + (1.0 - cosine)

    lost = lax.fori_loop(0, 2 * ROWS // 64, gradient, jnp.zeros((64, 1), F32))
    loss_out[...] = jnp.broadcast_to(jnp.sum(lost, axis=0, keepdims=True), (8, 128))

    def part(dj):
        return remote(part_send.at[dj], part_recv.at[dj], p_send.at[dj], p_recv.at[dj], peer)

    def result(dj):
        return remote(sum_send.at[dj], sum_recv.at[dj], r_send.at[dj], r_recv.at[dj], at.column(dj, 0))

    def produce(dj):
        weights = wbuf[(at.pipe + dj) % NP]
        part_send[dj] = nt(og_out[theirs, :], weights).astype(BF16)
        part(dj).start()
        part_mine[dj] = nt(og_out[mine, :], weights).astype(BF16)

    def send_on(dj):
        part(dj).wait_recv()
        sum_send[dj] = (part_mine[dj].astype(F32) + part_recv[dj].astype(F32)).astype(BF16)
        result(dj).start()

    steps = list(range(1, NP)) + [0]
    for k, dj in enumerate(steps):
        produce(dj)
        if k >= 1:
            send_on(steps[k - 1])
    part(0).wait_recv()
    for dj in range(1, NP):
        result(dj).wait_recv()

    @pl.loop(0, ROWS // 64)
    def _(step):
        rows = pl.ds(pl.multiple_of(step * 64, 64), 64)
        total = part_mine[0, rows, :].astype(F32) + part_recv[0, rows, :].astype(F32)
        for dj in range(1, NP):
            total = total + sum_recv[dj, rows, :].astype(F32)
        grad_out[rows, :] = total.astype(BF16)

    save.wait()
    peer_rows.wait_send()
    for dj in range(NP):
        forward(dj).wait_send()
        part(dj).wait_send()
    for dj in range(1, NP):
        share(dj).wait_send()
        result(dj).wait_send()
    for k in range(len(COLUMN)):
        stat(k).wait_send()


def middle(attended, wo, shallow, target):
    vmem = pl.BlockSpec(memory_space=pltpu.VMEM)
    anyspace = pl.BlockSpec(memory_space=pl.ANY)
    dma = pltpu.SemaphoreType.DMA
    blocks = pltpu.VMEM((NP, ROWS, BLK), BF16)
    return pl.pallas_call(
        middle_kernel,
        out_shape=(
            jax.ShapeDtypeStruct((ROWS, BLK), BF16),
            jax.ShapeDtypeStruct((NP, 2 * ROWS, BLK), BF16),
            jax.ShapeDtypeStruct((2 * ROWS, BLK), BF16),
            jax.ShapeDtypeStruct((8, 128), F32),
        ),
        in_specs=[vmem, anyspace, anyspace, vmem],
        out_specs=(vmem, anyspace, vmem, vmem),
        scratch_shapes=[
            pltpu.VMEM((NP, 2 * ROWS, BLK), BF16),
            pltpu.VMEM((NP, BLK, BLK), BF16),
            pltpu.VMEM((2 * ROWS, BLK), BF16),
            pltpu.VMEM((2 * ROWS, BLK), F32),
            pltpu.VMEM((2 * ROWS, 128), F32),
            pltpu.VMEM((128, 2 * ROWS), F32),
            pltpu.VMEM((8, 2 * ROWS), F32),
            pltpu.VMEM((15, 8, 2 * ROWS), F32),
            blocks, blocks, blocks, blocks, blocks,
            dma((NP,)), dma((NP,)), dma((NP,)), dma((NP,)), dma((15,)), dma((15,)),
            dma((NP,)), dma((NP,)), dma((NP,)), dma((NP,)), dma((1,)), dma((1,)), dma((3,)),
        ],
        compiler_params=pltpu.CompilerParams(
            collective_id=1, has_side_effects=True, vmem_limit_bytes=VLIM
        ),
        name="middle",
    )(attended, wo, shallow, target)


PLANES = [(dx, flip) for flip in (0, 1) for dx in range(NX) if (dx, flip) != (0, 0)]
N_REDUCE = 17


def tn(left, right):
    return lax.dot_general(
        left, right, (((0,), (0,)), ((), ())), preferred_element_type=F32
    )


class Reduce:
    def __init__(self, place, terms, corner, near, cross, cross_b, send_sems, recv_sems):
        self.place, self.terms = place, terms
        self.corner, self.near, self.cross, self.cross_b = corner, near, cross, cross_b
        self.send_sems, self.recv_sems = send_sems, recv_sems
        self.started = []

    def copy(self, k, dx, flip, row, rows, landing, device):
        source = self.terms.at[self.place.slot_of(dx, flip), pl.ds(row, rows)]
        return remote(source, landing, self.send_sems.at[k], self.recv_sems.at[k], device)

    def go(self, *what):
        copy = self.copy(*what)
        copy.start()
        self.started.append(copy)

    def wait(self, k, landing):
        remote(
            landing, landing, self.send_sems.at[k], self.recv_sems.at[k], self.place.plane(0, 1)
        ).wait_recv()

    def add(self, dx, flip, row, rows, *landings):
        slot = self.place.slot_of(dx, flip)

        @pl.loop(0, rows // 32)
        def _(step):
            low = pl.multiple_of(step * 32, 32)
            here = pl.ds(pl.multiple_of(row + low, 32), 32)
            total = self.terms[slot, here, :].astype(F32)
            for landing in landings:
                total = total + landing[pl.ds(low, 32), :].astype(F32)
            self.terms[slot, here, :] = total.astype(BF16)

    def x_begin(self, n):
        flip, row = (n, 0) if n < 2 else (0, HALF)
        self.go(4 * n, 2, flip, row, QUART, self.corner.at[n, 0], self.place.plane(1, 0))
        self.go(4 * n + 1, 2, flip, row + QUART, QUART, self.corner.at[n, 1], self.place.plane(-1, 0))

    def x_pass(self, n):
        flip, row = (n, 0) if n < 2 else (0, HALF)
        self.wait(4 * n, self.corner.at[n, 0])
        self.add(1, flip, row, QUART, self.corner.at[n, 0])
        self.go(4 * n + 2, 1, flip, row, HALF, self.near.at[n, 0], self.place.plane(1, 0))
        self.wait(4 * n + 1, self.corner.at[n, 1])
        self.add(-1, flip, row + QUART, QUART, self.corner.at[n, 1])
        self.go(4 * n + 3, -1, flip, row, HALF, self.near.at[n, 1], self.place.plane(-1, 0))

    def x_end(self, n):
        flip, row = (n, 0) if n < 2 else (0, HALF)
        self.wait(4 * n + 2, self.near.at[n, 0])
        self.wait(4 * n + 3, self.near.at[n, 1])
        self.add(0, flip, row, HALF, self.near.at[n, 0], self.near.at[n, 1])

    def z_second(self, dx):
        self.go(13 + dx, dx, 1, HALF, HALF, self.cross_b.at[dx], self.place.plane(0, 1))

    def z_second_add(self, dx):
        self.wait(13 + dx, self.cross_b.at[dx])
        self.add(dx, 0, HALF, HALF, self.cross_b.at[dx])

    def begin(self):
        self.z_second(2)
        self.x_begin(1)
        self.x_begin(0)
        for dx in (1, 3, 0):
            self.z_second(dx)

    def middle(self):
        self.x_pass(1)
        self.z_second_add(2)
        self.x_begin(2)
        self.x_pass(0)
        self.z_second_add(1)
        self.z_second_add(3)
        self.x_pass(2)

    def late(self):
        self.x_end(1)
        self.go(12, 0, 1, 0, HALF, self.cross, self.place.plane(0, 1))
        self.x_end(0)
        self.z_second_add(0)

    def finish(self):
        self.x_end(2)
        self.wait(12, self.cross)
        self.add(0, 0, 0, HALF, self.cross)

    def drain(self):
        for copy in self.started:
            copy.wait_send()


def squares_of(read, rows, width):
    def step(k, total):
        v = read(pl.ds(pl.multiple_of(k * 32, 32), 32)).astype(F32)
        v = jnp.sum((v * v).reshape(4, 8, width), axis=0)
        for first in range(0, width, 128):
            total = total + v[:, first:first + 128]
        return total

    return lax.fori_loop(0, rows // 32, step, jnp.zeros((8, 128), F32))


def back_kernel(
    normed, att_all, og, q_grad, kv_part, cosine, sine, loss,
    gq_out, go_out, stat_out,
    nbuf, abuf, both, kv_recv, o_terms, o_corner, o_near, o_cross, o_cross_b,
    q_terms, q_corner, q_near, q_cross, q_cross_b, stat_one, stat_two, from_column, from_plane,
    o_send, o_recv, q_send, q_recv, k_send, k_recv, g_send, g_recv, s_send, s_recv,
    c_send, c_recv, p_send, p_recv, local_sems,
):
    at = Place()
    greet([at.plane(*d) for d in PLANES] + [at.column(*d) for d in COLUMN], at)
    peer = at.column(0, 1)
    mine = pl.ds(pl.multiple_of(at.c * ROWS, ROWS), ROWS)
    theirs = pl.ds(pl.multiple_of(at.o * ROWS, ROWS), ROWS)

    def kv_copy(dj):
        return remote(
            kv_part.at[(at.pipe + dj) % NP], kv_recv.at[dj], k_send.at[dj], k_recv.at[dj],
            at.column(dj, 0),
        )

    for dj in range(1, NP):
        kv_copy(dj).start()
    load_att = pltpu.make_async_copy(att_all, abuf, local_sems.at[0])
    load_att.start()
    load_normed = pltpu.make_async_copy(normed, nbuf, local_sems.at[1])
    load_normed.start()

    load_att.wait()

    @pl.loop(0, NP)
    def _(k):
        o_terms[k] = tn(abuf[k], og[...]).astype(BF16)

    out_reduce = Reduce(at, o_terms, o_corner, o_near, o_cross, o_cross_b, o_send, o_recv)
    query_reduce = Reduce(at, q_terms, q_corner, q_near, q_cross, q_cross_b, q_send, q_recv)
    out_reduce.begin()

    total = kv_part[at.pipe].astype(F32)
    for dj in range(1, NP):
        kv_copy(dj).wait_recv()
        total = total + kv_recv[dj].astype(F32)
    is_key = (at.pipe % 2 == 0).astype(F32)
    total = turned(total, cosine[...], -sine[...]) * is_key + total * (1.0 - is_key)
    both[mine, pl.ds(0, BLK)] = q_grad[...]
    both[mine, pl.ds(BLK, HD)] = total.astype(BF16)
    exchange = remote(both.at[mine], both.at[mine], g_send.at[0], g_recv.at[0], peer)
    exchange.start()
    load_normed.wait()
    remote(both.at[theirs], both.at[theirs], g_send.at[0], g_recv.at[0], peer).wait_recv()

    @pl.loop(0, NP)
    def _(k):
        q_terms[k] = tn(nbuf[k], both[...]).astype(BF16)

    out_reduce.middle()
    query_reduce.begin()
    out_reduce.late()
    out_reduce.finish()

    own = at.slot
    swap = remote(o_terms.at[own], go_out, s_send.at[0], s_recv.at[0], at.swap())
    keep = pltpu.make_async_copy(o_terms.at[own], go_out, local_sems.at[2])

    @pl.when(at.swaps)
    def _():
        swap.start()

    @pl.when(jnp.logical_not(at.swaps))
    def _():
        keep.start()

    tile = squares_of(lambda rows: o_terms[own, rows, :], BLK, BLK)
    query_reduce.middle()
    query_reduce.late()
    query_reduce.finish()
    gq_out[...] = q_terms[own]
    stat_one[pl.ds(0, 8), :] = tile + squares_of(lambda rows: q_terms[own, rows, :], BLK, WQ)
    stat_one[pl.ds(8, 8), :] = loss[...]

    def column_copy(k):
        return remote(stat_one, from_column.at[k], c_send.at[k], c_recv.at[k], at.column(*COLUMN[k]))

    def plane_copy(k):
        return remote(stat_two, from_plane.at[k], p_send.at[k], p_recv.at[k], at.plane(*PLANES[k]))

    for k in range(len(COLUMN)):
        column_copy(k).start()
    total = stat_one[...]
    for k in range(len(COLUMN)):
        column_copy(k).wait_recv()
        total = total + from_column[k]
    stat_two[...] = total
    for k in range(len(PLANES)):
        plane_copy(k).start()
    for k in range(len(PLANES)):
        plane_copy(k).wait_recv()
        total = total + from_plane[k]
    stat_out[...] = total

    @pl.when(at.swaps)
    def _():
        swap.wait_recv()
        swap.wait_send()

    @pl.when(jnp.logical_not(at.swaps))
    def _():
        keep.wait()

    out_reduce.drain()
    query_reduce.drain()
    exchange.wait_send()
    for dj in range(1, NP):
        kv_copy(dj).wait_send()
    for k in range(len(COLUMN)):
        column_copy(k).wait_send()
    for k in range(len(PLANES)):
        plane_copy(k).wait_send()


def back(normed, att_all, og, q_grad, kv_part, cosine, sine, loss):
    vmem = pl.BlockSpec(memory_space=pltpu.VMEM)
    anyspace = pl.BlockSpec(memory_space=pl.ANY)
    dma = pltpu.SemaphoreType.DMA

    def buffers(width):
        return [
            pltpu.VMEM((NP, BLK, width), BF16),
            pltpu.VMEM((3, 2, QUART, width), BF16),
            pltpu.VMEM((3, 2, HALF, width), BF16),
            pltpu.VMEM((HALF, width), BF16),
            pltpu.VMEM((4, HALF, width), BF16),
        ]

    return pl.pallas_call(
        back_kernel,
        out_shape=(
            jax.ShapeDtypeStruct((BLK, WQ), BF16),
            jax.ShapeDtypeStruct((BLK, BLK), BF16),
            jax.ShapeDtypeStruct((16, 128), F32),
        ),
        in_specs=[anyspace, anyspace, vmem, vmem, vmem, vmem, vmem, vmem],
        out_specs=(vmem, vmem, vmem),
        scratch_shapes=[
            pltpu.VMEM((NP, 2 * ROWS, BLK), BF16),
            pltpu.VMEM((NP, 2 * ROWS, BLK), BF16),
            pltpu.VMEM((2 * ROWS, WQ), BF16),
            pltpu.VMEM((NP, ROWS, HD), BF16),
            *buffers(BLK), *buffers(WQ),
            pltpu.VMEM((16, 128), F32),
            pltpu.VMEM((16, 128), F32),
            pltpu.VMEM((15, 16, 128), F32),
            pltpu.VMEM((7, 16, 128), F32),
            dma((N_REDUCE,)), dma((N_REDUCE,)), dma((N_REDUCE,)), dma((N_REDUCE,)),
            dma((NP,)), dma((NP,)), dma((1,)), dma((1,)), dma((1,)), dma((1,)),
            dma((15,)), dma((15,)), dma((7,)), dma((7,)), dma((3,)),
        ],
        compiler_params=pltpu.CompilerParams(
            collective_id=2, has_side_effects=True, vmem_limit_bytes=VLIM
        ),
        name="back",
    )(normed, att_all, og, q_grad, kv_part, cosine, sine, loss)


def rotary_tables(positions):
    half_width = HD // 2
    exponent = jnp.arange(half_width).astype(F32) * (2.0 / HD)
    inverse = jnp.power(jnp.float32(theta_base), -exponent)
    angle_table = positions.astype(F32)[:, None] * inverse[None, :]
    cosine, sine = jnp.cos(angle_table), jnp.sin(angle_table)
    return jnp.concatenate([cosine, cosine], axis=1), jnp.concatenate([-sine, sine], axis=1)


def attend(queries, keys_head, values_head, allowed):
    score_scale = 1.0 / math.sqrt(queries.shape[-1])
    scores = (
        jnp.einsum("rhd,khd->hrk", queries, keys_head, preferred_element_type=F32) * score_scale
    )
    scores = jnp.where(allowed[None], scores, mask_fill)
    highest = jnp.max(scores, axis=-1, keepdims=True)
    weights = jnp.exp(scores - highest)
    softmax_rows = weights / jnp.sum(weights, axis=-1, keepdims=True)
    softmax_low = softmax_rows.astype(BF16)
    attended = jnp.einsum(
        "hrk,khd->rhd", softmax_low, values_head, preferred_element_type=F32
    ).astype(BF16)
    return (softmax_rows, softmax_low, attended)


def attend_grad(softmax_rows, softmax_low, queries, keys_head, values_head, att_grad):
    score_scale = 1.0 / math.sqrt(queries.shape[-1])
    inner_prod = jnp.einsum("rhd,khd->hrk", att_grad, values_head, preferred_element_type=F32)
    centred = inner_prod - jnp.sum(softmax_rows * inner_prod, axis=-1, keepdims=True)
    score_grad = (softmax_rows * centred * score_scale).astype(BF16)
    query_part = jnp.einsum("hrk,khd->rhd", score_grad, keys_head, preferred_element_type=F32)
    key_part = jnp.einsum("hrk,rhd->hkd", score_grad, queries, preferred_element_type=F32)
    value_part = jnp.einsum("hrk,rhd->hkd", softmax_low, att_grad, preferred_element_type=F32)
    return (query_part, key_part, value_part)


def per_device(shallow, teacher, positions, segments, in_gain, w_query, w_keyval, w_output):
    heads = BLK // HD
    all_rows = ROWS * lax.axis_size("dp")
    param_count = D * (2 * QH * HD + 2 * KV * HD)
    cosine, sine = rotary_tables(positions)
    queries, keyvals, normed, wo, target = front(
        shallow, in_gain[None], w_query, w_keyval, w_output, teacher, cosine, sine
    )
    queries = queries.reshape(ROWS, heads, HD)
    keyvals = keyvals.reshape(KV, 2, ROWS, HD)
    keys_head = keyvals[:, 0].transpose(1, 0, 2)
    values_head = keyvals[:, 1].transpose(1, 0, 2)
    row_order = jnp.arange(ROWS)
    allowed = (segments[:, None] == segments[None, :]) & (row_order[None, :] <= row_order[:, None])
    softmax_rows, softmax_low, attended = attend(queries, keys_head, values_head, allowed)
    att_grad, att_all, out_grad, loss = middle(
        attended.reshape(ROWS, BLK), wo, shallow, target.reshape(2 * ROWS, BLK)
    )
    query_part, key_part, value_part = attend_grad(
        softmax_rows, softmax_low, queries, keys_head, values_head, att_grad.reshape(ROWS, heads, HD)
    )
    half = HD // 2
    rolled = jnp.concatenate([query_part[..., half:], query_part[..., :half]], axis=-1)
    query_grad = (query_part * cosine[:, None] - rolled * sine[:, None]).astype(BF16)
    kv_part = jnp.stack([key_part, value_part], axis=1).astype(BF16).reshape(2 * KV, ROWS, HD)
    grad_qkv, grad_output, stats = back(
        normed, att_all, out_grad, query_grad.reshape(ROWS, BLK), kv_part, cosine, sine, loss
    )
    square_total = jnp.sum(stats[:8])
    inverse = 1.0 / jnp.sqrt(square_total / param_count + mean_eps)
    loss_total = stats[8, 0] / lax.axis_size("pipe") / 2
    grad_qkv = grad_qkv.astype(F32)
    return (
        loss_total / all_rows,
        grad_qkv[:, :BLK] * inverse,
        grad_qkv[:, BLK:] * inverse,
        grad_output.astype(F32) * inverse,
    )


def solution(mesh):
    placed = (
        P("dp", None),
        P(("dp", "pipe"), None),
        P("dp"),
        P("dp"),
        P(),
        P("dp", "pipe"),
        P("dp", "pipe"),
        P("pipe", "dp"),
    )
    return jax.shard_map(
        per_device,
        mesh=mesh,
        in_specs=placed,
        out_specs=(P(), P("dp", "pipe"), P("dp", "pipe"), P("pipe", "dp")),
        check_vma=False,
    )
```

time: 726 us -> 354 us (0.49)
  waiting for transfers between devices: 525 us -> 0 us
  Pallas kernels: 0 us -> 329 us
  blocking collectives: 94 us -> 0 us
  matrix products: 46.8 us -> 8.66 us
  other arithmetic: 31.7 us -> 7.73 us
  between operations: 18.8 us -> 3.35 us
    reduce_scatter x3 -> x0, waiting for transfers between devices: 331 us -> none  [the longest x1 203 us: per_device(): lax.psum_scatter(jnp.concatenate([contract_rows(columns, grad_inputs), co...]
    pallas_call x0 -> x3, Pallas kernels: none -> 329 us  [the longest x1 133 us: back(): pl.pallas_call(back_kernel, out_shape=(jax.ShapeDtypeStruct((BLK, WQ), BF...]
    all_gather x4 -> x0, waiting for transfers between devices: 176 us -> none  [the longest x1 71 us: per_device(): grad_all = lax.all_gather(out_grad, 'pipe', axis=0, tiled=True)]
    psum x1 -> x0, blocking collectives: 64.6 us -> none  [per_device(): loss_total = lax.psum(loss_local, ('dp', 'pipe'))]
    dot_general x10 -> x2, matrix products: 43.5 us -> 3.5 us  [the longest x1 1.99 us: attend_grad(): jnp.einsum('hrk,rhd->hkd', score_grad, queries, preferred_element_type=F32)]
    all_gather x1 -> x0, blocking collectives: 29.5 us -> none  [per_device(): lax.all_gather(keyval_local.reshape(group_rows, keyval_cols), 'pipe', axi...]
    ppermute x1 -> x0, waiting for transfers between devices: 15.5 us -> none  [shifted(): return lax.ppermute(value, axis, pairs)]
    concatenate x4 -> x1, other arithmetic: 14.6 us -> 0.83 us  [rotary_tables(): jnp.concatenate([cosine, cosine], axis=1)]
  transfers between devices with their start and end apart: 8 -> 0, of which waited for: 8 -> 0; matrix products, arithmetic and copies ran while one was open for 4% -> 0% of each run, Pallas kernels for 0% -> 0%
where the time goes in v1:
time: 354 us
  Pallas kernels  329 us (93%)
  matrix products  8.66 us (2%)
  other arithmetic  7.73 us (2%)
  local copies, waits for them, and re-layouts  5.14 us (1%)
    pallas_call x1, Pallas kernels, back(): pl.pallas_call(back_kernel, out_shape=(jax.ShapeDtypeStruct((BLK, WQ), BF...  133 us
    pallas_call x1, Pallas kernels, front(): pl.pallas_call(front_kernel, out_shape=(jax.ShapeDtypeStruct((ROWS, BLK),...  107 us
    pallas_call x1, Pallas kernels, middle(): pl.pallas_call(middle_kernel, out_shape=(jax.ShapeDtypeStruct((ROWS, BLK)...  88.7 us

profile of v1, /device:TPU:1, one launch (start us, length us, event | category | flops | bytes accessed | tf_op | source)
XLA Modules:
  0.0 353.9 jit_solution(1263548339497959327)
XLA Ops:
  0.7 0.7 convert_element_type.36
  1.3 0.5 fusion.36
  1.9 0.8 pad_maximum_fusion.1
  2.7 107.4 %front.1 = (bf16[256,512]{1,0:T(8,128)(2,1)}, bf16[8,256,128]{2,1,0:T(8,128)(2,1)}, bf16[8,512,512]{2,1,0:T(8,128)(2,1)}, bf16[8,512,512]{2,1,0:T(8,128)(2,1)}, bf16[2,8,32,512]{3,2,1,0:T(8,128)(2,1)}) custom-call(bf16[256,8192]{1,0:T(8,128)(2,1)} %shallow.3, f32[1,8192]{1,0:T(1,128)} %bitcast.74, bf16[512,512]{1,0:T(8,128)(2,1)} %wq.1, ...), custom_call_target="tpu_custom_call" | custom-call | tf_op jit(solution)/shard_map/front/pallas_call | solution.py:341
  110.1 1.0 slice.32
  111.1 0.1 copy.33
  111.4 1.5 fusion.47
  112.9 0.2 convolution_convert_fusion.2
  113.1 0.8 copy.31.attended
  114.0 88.7 %middle.1 = (bf16[256,512]{1,0:T(8,128)(2,1)}, bf16[8,512,512]{2,1,0:T(8,128)(2,1)}, bf16[512,512]{1,0:T(8,128)(2,1)}, f32[8,128]{1,0:T(8,128)}) custom-call(bf16[256,512]{1,0:T(8,128)(2,1)} %copy.31.attended, bf16[8,512,512]{2,1,0:T(8,128)(2,1)} %get-tuple-element.19.wo, bf16[256,8192]{1,0:T(8,128)(2,1)} %shallow.3, bf16[512,512]{1,0:T(8,128)(2,1)} %bitcast.69), custom_call_target="tpu_custom_call" | custom-call | tf_op jit(solution)/shard_map/middle/pallas_call | solution.py:540
  202.7 1.3 fusion.21
  204.1 2.1 convolution_bitcast_fusion
  206.4 0.1 fusion.17
  206.5 0.8 copy.32.q_grad
  207.4 1.5 fusion.10
  208.9 2.0 fusion.9
  211.0 0.8 copy.26
  211.8 133.0 %back.1 = (bf16[512,640]{1,0:T(8,128)(2,1)}, bf16[512,512]{1,0:T(8,128)(2,1)}, f32[16,128]{1,0:T(8,128)}) custom-call(bf16[8,512,512]{2,1,0:T(8,128)(2,1)} %get-tuple-element.16.normed, bf16[8,512,512]{2,1,0:T(8,128)(2,1)} %get-tuple-element.21.att_all, bf16[512,512]{1,0:T(8,128)(2,1)} %get-tuple-element.22.og, bf16[256,512]{1,0:T(8,128)(2,1)} %copy.32.q_grad, ...), custom_call_target="tpu_custom_call" | custom-call | tf_op jit(solution)/shard_map/back/pallas_call | solution.py:816
  344.8 1.2 slice.28
  346.7 1.2 convert_element_type.44
  347.9 1.3 slice_reduce_fusion
  349.9 1.1 slice_multiply_fusion
  351.0 0.7 slice_multiply_fusion.1
  351.7 1.1 convert_multiply_fusion
  (22 shorter events, 0.4 us)
Async XLA Ops:
  0.6 110.6 %copy-start.5 = (s32[256]{0:T(256)S(1)}, s32[256]{0:T(256)}, u32[]{:S(2)}) copy-start(s32[256]{0:T(256)} %param.11) | copy-start | bytes 3076
  112.9 89.8 %copy-start.7 = (f32[4,256,256]{1,2,0:T(8,128)}, f32[4,256,256]{1,2,0:T(8,128)S(1)}, u32[]{:S(2)}) copy-start(f32[4,256,256]{1,2,0:T(8,128)S(1)} %get-tuple-element.34) | copy-start | bytes 3145732
  114.0 90.1 %copy-start.4 = (bf16[8,256,128]{2,1,0:T(8,128)(2,1)S(1)}, bf16[8,256,128]{2,1,0:T(8,128)(2,1)}, u32[]{:S(2)}) copy-start(bf16[8,256,128]{2,1,0:T(8,128)(2,1)} %get-tuple-element.17) | copy-start | bytes 1572868
  202.7 3.5 copy-start.1
  202.7 3.6 %copy-start = (f32[256,128]{1,0:T(8,128)S(1)}, f32[256,128]{1,0:T(8,128)}, u32[]{:S(2)}) copy-start(f32[256,128]{1,0:T(8,128)} %get-tuple-element.35.cosine) | copy-start | bytes 393220
  204.1 3.3 copy-start.3
  206.2 2.8 copy-start.6
  344.8 6.9 %copy-start.2 = (bf16[512,512]{1,0:T(8,128)(2,1)S(1)}, bf16[512,512]{1,0:T(8,128)(2,1)}, u32[]{:S(2)}) copy-start(bf16[512,512]{1,0:T(8,128)(2,1)} %get-tuple-element.27) | copy-start | bytes 1572868

commit v2 on v0

v2 whole, which is shorter than its diff:
```python
import functools
import math

import jax
import jax.numpy as jnp
from jax import lax
from jax.experimental import pallas as pl
from jax.experimental.pallas import tpu as pltpu
from jax.sharding import PartitionSpec as P

D = 8192
HD = 128
QH = 32
KV = 4
NP = 8
NX = 4
BLK = 512
ROWS = 256
WQ = 640

theta_base = 10000.0
norm_eps = 1e-05
cosine_eps = 1e-06
mean_eps = 1e-12
mask_fill = -1e30

MESH = pl.DeviceIdType.MESH
F32 = jnp.float32
BF16 = jnp.bfloat16
VLIM = 60 * 1024 * 1024


def remote(src, dst, send_sem, recv_sem, device):
    return pltpu.make_async_remote_copy(
        src_ref=src, dst_ref=dst, send_sem=send_sem, recv_sem=recv_sem,
        device_id=device, device_id_type=MESH,
    )


class Place:
    def __init__(self):
        dp = lax.axis_index("dp")
        self.dp = dp
        self.pipe = lax.axis_index("pipe")
        self.x = dp // 4
        self.z = (dp // 2) % 2
        self.c = dp % 2
        self.o = 1 - self.c
        self.y = self.pipe // 2
        self.high = self.pipe % 2
        self.slot = dp // 2
        self.swaps = self.slot != self.pipe

    def slot_of(self, axis, dx, flip):
        along, z = (self.x, self.z) if axis == "dp" else (self.y, self.high)
        return (along + dx + NX) % NX * 2 + (1 - z if flip else z)

    def near(self, axis, dx, flip):
        slot = self.slot_of(axis, dx, flip)
        return (slot * 2 + self.c, self.pipe) if axis == "dp" else (self.dp, slot)

    def cross(self, dx, flip, other):
        return (self.slot_of("dp", dx, flip) * 2 + (self.o if other else self.c), self.pipe)

    def column(self, dj, other):
        return (self.slot * 2 + (self.o if other else self.c), (self.pipe + dj) % NP)

    def swap(self):
        return (self.pipe * 2 + self.c, self.slot)


COLUMN = [(dj, other) for other in (0, 1) for dj in range(NP) if (dj, other) != (0, 0)]
PLANES = [(dx, flip) for flip in (0, 1) for dx in range(NX) if (dx, flip) != (0, 0)]
GROUP = [
    (dx, flip, other) for other in (0, 1) for flip in (0, 1) for dx in range(NX)
    if (dx, flip, other) != (0, 0, 0)
]


def greet(at):
    barrier = pltpu.get_barrier_semaphore()
    devices = [at.cross(*d) for d in GROUP] + [at.column(*d) for d in COLUMN]
    for device in devices:
        pl.semaphore_signal(barrier, inc=1, device_id=device, device_id_type=MESH)

    @pl.when(at.swaps)
    def _():
        pl.semaphore_signal(barrier, inc=1, device_id=at.swap(), device_id_type=MESH)

    pl.semaphore_wait(barrier, len(devices) + at.swaps.astype(jnp.int32))


FIRST = {
    "a_z": (0, 0, 0, 2, "z"),
    "a_xp": (0, 0, 0, 2, "p"),
    "a_xm": (0, 0, 0, 2, "m"),
    "a_fp": (-1, 0, 0, 1, "p"),
    "a_fm": (1, 0, 1, 1, "m"),
    "az_xp": (0, 1, 0, 2, "p"),
    "az_xm": (0, 1, 0, 2, "m"),
    "az_fp": (-1, 1, 0, 1, "p"),
    "az_fm": (1, 1, 1, 1, "m"),
}
SECOND = {
    "b_xp": (0, 0, 2, 2, "p"),
    "b_xm": (0, 0, 2, 2, "m"),
    "b_fp": (-1, 0, 2, 1, "p"),
    "b_fm": (1, 0, 3, 1, "m"),
    "b_z0": (0, 0, 2, 2, "z"),
    "b_zm": (-1, 0, 2, 2, "z"),
    "b_zp": (1, 0, 2, 2, "z"),
    "b_z2a": (2, 0, 2, 1, "z"),
    "b_z2b": (2, 0, 3, 1, "z"),
}
N_GATHER = len(FIRST) + len(SECOND)
N_FIRST = len(FIRST)


class Gather:
    def __init__(self, at, axis, view, rows, send_sems, recv_sems, halves):
        self.at, self.axis, self.view = at, axis, view
        self.send_sems, self.recv_sems = send_sems, recv_sems
        self.halves = halves
        self.table = {**FIRST, **SECOND} if halves else FIRST
        self.part = rows // 4 if halves else rows // 2
        self.order = {name: k for k, name in enumerate(self.table)}

    def copy(self, name, dx, flip):
        _, _, first, parts, way = self.table[name]
        k = self.order[name]
        region = self.view(
            self.at.slot_of(self.axis, dx, flip), first * self.part, parts * self.part
        )
        device = {
            "p": self.at.near(self.axis, 1, 0),
            "m": self.at.near(self.axis, -1, 0),
            "z": self.at.near(self.axis, 0, 1),
        }[way]
        return remote(region, region, self.send_sems.at[k], self.recv_sems.at[k], device)

    def out(self, name):
        return self.copy(name, self.table[name][0], self.table[name][1])

    def start(self, *names):
        for name in names:
            self.out(name).start()

    def wait(self, *names):
        for name in names:
            dx, flip, _, _, way = self.table[name]
            dx = dx + {"p": -1, "m": 1, "z": 0}[way]
            self.copy(name, dx, 1 - flip if way == "z" else flip).wait_recv()

    def begin(self):
        self.start("a_z", "a_xp", "a_xm")
        if self.halves:
            self.start("b_xp", "b_xm", "b_z0")

    def middle(self):
        self.wait("a_z")
        self.start("az_xp", "az_xm")
        self.wait("a_xp")
        self.start("a_fp")
        self.wait("a_xm")
        self.start("a_fm")
        if self.halves:
            self.wait("b_xp")
            self.start("b_fp", "b_zm")
            self.wait("b_xm")
            self.start("b_fm", "b_zp")

    def late(self):
        self.wait("az_xp")
        self.start("az_fp")
        self.wait("az_xm")
        self.start("az_fm")
        if self.halves:
            self.wait("b_fp")
            self.start("b_z2a")
            self.wait("b_fm")
            self.start("b_z2b")

    def finish(self):
        self.wait("a_fp", "a_fm", "az_fp", "az_fm")
        if self.halves:
            self.wait("b_z0", "b_zm", "b_zp", "b_z2a", "b_z2b")

    def drain(self):
        for name in self.table:
            self.out(name).wait_send()


N_REDUCE = 17
N_REDUCE_FIRST = 9


class Reduce:
    def __init__(self, at, axis, terms, rows, corner, near, cross, cross_b, send_sems, recv_sems):
        self.at, self.axis, self.terms = at, axis, terms
        self.corner, self.near, self.cross, self.cross_b = corner, near, cross, cross_b
        self.send_sems, self.recv_sems = send_sems, recv_sems
        self.half = rows if cross_b is None else rows // 2
        self.quarter = self.half // 2
        self.started = []

    def go(self, k, dx, flip, row, rows, landing, device):
        source = self.terms.at[self.at.slot_of(self.axis, dx, flip), pl.ds(row, rows)]
        copy = remote(
            source, landing, self.send_sems.at[k], self.recv_sems.at[k],
            self.at.near(self.axis, *device),
        )
        copy.start()
        self.started.append(copy)

    def wait(self, k, landing):
        remote(
            landing, landing, self.send_sems.at[k], self.recv_sems.at[k],
            self.at.near(self.axis, 0, 1),
        ).wait_recv()

    def add(self, dx, flip, row, rows, *landings):
        slot = self.at.slot_of(self.axis, dx, flip)

        @pl.loop(0, rows // 32)
        def _(step):
            low = pl.multiple_of(step * 32, 32)
            here = pl.ds(pl.multiple_of(row + low, 32), 32)
            total = self.terms[slot, here, :].astype(F32)
            for landing in landings:
                total = total + landing[pl.ds(low, 32), :].astype(F32)
            self.terms[slot, here, :] = total.astype(BF16)

    def where(self, n):
        return (n, 0) if n < 2 else (0, self.half)

    def x_begin(self, n):
        flip, row = self.where(n)
        quarter = self.quarter
        self.go(4 * n, 2, flip, row, quarter, self.corner.at[n, 0], (1, 0))
        self.go(4 * n + 1, 2, flip, row + quarter, quarter, self.corner.at[n, 1], (-1, 0))

    def x_pass(self, n):
        flip, row = self.where(n)
        quarter = self.quarter
        self.wait(4 * n, self.corner.at[n, 0])
        self.add(1, flip, row, quarter, self.corner.at[n, 0])
        self.go(4 * n + 2, 1, flip, row, self.half, self.near.at[n, 0], (1, 0))
        self.wait(4 * n + 1, self.corner.at[n, 1])
        self.add(-1, flip, row + quarter, quarter, self.corner.at[n, 1])
        self.go(4 * n + 3, -1, flip, row, self.half, self.near.at[n, 1], (-1, 0))

    def x_end(self, n):
        flip, row = self.where(n)
        self.wait(4 * n + 2, self.near.at[n, 0])
        self.wait(4 * n + 3, self.near.at[n, 1])
        self.add(0, flip, row, self.half, self.near.at[n, 0], self.near.at[n, 1])

    @property
    def z_sem(self):
        return 8 if self.cross_b is None else 12

    def z_first(self):
        self.go(self.z_sem, 0, 1, 0, self.half, self.cross, (0, 1))

    def z_first_add(self):
        self.wait(self.z_sem, self.cross)
        self.add(0, 0, 0, self.half, self.cross)

    def z_second(self, dx):
        self.go(13 + dx, dx, 1, self.half, self.half, self.cross_b.at[dx], (0, 1))

    def z_second_add(self, dx):
        self.wait(13 + dx, self.cross_b.at[dx])
        self.add(dx, 0, self.half, self.half, self.cross_b.at[dx])

    def begin(self):
        self.z_second(2)
        self.x_begin(1)
        self.x_begin(0)
        for dx in (1, 3, 0):
            self.z_second(dx)

    def middle(self):
        self.x_pass(1)
        self.z_second_add(2)
        self.x_begin(2)
        self.x_pass(0)
        self.z_second_add(1)
        self.z_second_add(3)
        self.x_pass(2)

    def late(self):
        self.x_end(1)
        self.z_first()
        self.x_end(0)
        self.z_second_add(0)

    def finish(self):
        self.x_end(2)
        self.z_first_add()

    def drain(self):
        for copy in self.started:
            copy.wait_send()


def nt(left, right):
    return lax.dot_general(
        left, right, (((1,), (1,)), ((), ())), preferred_element_type=F32
    )


def tn(left, right):
    return lax.dot_general(
        left, right, (((0,), (0,)), ((), ())), preferred_element_type=F32
    )


def turned(v, cosine, sine):
    half = HD // 2
    rolled = jnp.concatenate([v[:, half:], v[:, :half]], axis=1)
    return v * cosine + rolled * sine


def squares_of(read, rows, width):
    def step(k, total):
        v = read(pl.ds(pl.multiple_of(k * 32, 32), 32)).astype(F32)
        v = jnp.sum((v * v).reshape(4, 8, width), axis=0)
        for first in range(0, width, 128):
            total = total + v[:, first:first + 128]
        return total

    return lax.fori_loop(0, rows // 32, step, jnp.zeros((8, 128), F32))


def aligned(start, size):
    return pl.ds(pl.multiple_of(start, size), size)


def step_kernel(
    shallow, gain, wq, wkv, wo, teacher, cosine, sine, seg_column, seg_row,
    gq_out, go_out, stat_out,
    wbuf, obuf, nbuf, pbuf, tbuf, target, acc, sum_mine, sum_theirs, qbuf, kvbuf, probs,
    abuf, sbuf, ogbuf, lanes, square, stat_send, stat_recv,
    part_send, part_recv, g_terms, g_corner, g_near, g_cross,
    kv_part, kv_recv, o_terms, o_corner, o_near, o_cross, o_cross_b,
    qgbuf, stat_one, stat_two, from_column, from_plane,
    w_send, w_recv, o_send, o_recv, n_send, n_recv, x_send, x_recv, m_send, m_recv,
    t_send, t_recv, k_send, k_recv, swap_send, swap_recv,
    a_send, a_recv, f_send, f_recv, s_send, s_recv, p_send, p_recv, r_send, r_recv,
    d_send, d_recv, e_send, e_recv, q_send, q_recv, h_send, h_recv,
    c_send, c_recv, l_send, l_recv, local_sems,
):
    at = Place()
    mine = aligned(at.c * ROWS, ROWS)
    theirs = aligned(at.o * ROWS, ROWS)
    heads = BLK // HD
    greet(at)
    peer = at.column(0, 1)
    is_key = (at.pipe % 2 == 0).astype(F32)

    def slots(buf):
        return lambda slot, row, rows: buf.at[slot, pl.ds(row, rows)]

    def slots_mine(buf):
        return lambda slot, row, rows: buf.at[slot, aligned(at.c * ROWS + row, rows)]

    wg = Gather(at, "dp", slots(wbuf), BLK, w_send, w_recv, True)
    og = Gather(at, "dp", slots(obuf), BLK, o_send, o_recv, True)
    ng = Gather(
        at, "pipe", lambda slot, row, rows: tbuf.at[pl.ds(row, rows), aligned(slot * 32, 32)],
        16, m_send, m_recv, False,
    )
    ag = Gather(at, "pipe", slots_mine(abuf), ROWS, a_send, a_recv, False)
    qg = Gather(at, "dp", slots_mine(qgbuf), ROWS, q_send, q_recv, True)

    wbuf[at.slot, :, pl.ds(0, BLK)] = wq[...]
    wbuf[at.slot, :, pl.ds(BLK, HD)] = wkv[...]
    wg.begin()

    swap = remote(wo, obuf.at[at.pipe], swap_send.at[0], swap_recv.at[0], at.swap())
    keep = pltpu.make_async_copy(wo, obuf.at[at.pipe], local_sems.at[0])

    @pl.when(at.swaps)
    def _():
        swap.start()

    @pl.when(jnp.logical_not(at.swaps))
    def _():
        keep.start()

    def target_copy(k):
        dj, other = COLUMN[k]
        block = (at.pipe + dj) % NP * 2 + (at.o if other else at.c)
        return remote(
            teacher.at[:, aligned(block * BLK, BLK)],
            target.at[at.c, (at.pipe + 1) % NP],
            t_send.at[k], t_recv.at[k], at.column(dj, other),
        )

    def target_arrival(k):
        dj, other = COLUMN[k]
        region = target.at[at.o if other else at.c, (at.pipe - dj + NP + 1) % NP]
        return remote(region, region, t_send.at[k], t_recv.at[k], peer)

    for k in range(len(COLUMN)):
        target_copy(k).start()
    own_block = aligned((at.pipe * 2 + at.c) * BLK, BLK)
    peer_block = aligned((at.pipe * 2 + at.o) * BLK, BLK)
    own_target = pltpu.make_async_copy(
        teacher.at[:, own_block], target.at[at.c, (at.pipe + 1) % NP], local_sems.at[1]
    )
    own_target.start()
    own_rows = pltpu.make_async_copy(shallow.at[:, own_block], sbuf.at[mine], local_sems.at[2])
    own_rows.start()
    peer_rows = remote(shallow.at[:, peer_block], sbuf.at[mine], h_send.at[8], h_recv.at[8], peer)
    peer_rows.start()

    @pl.loop(0, ROWS // 32)
    def _(step):
        rows = aligned(step * 32, 32)

        def squares(k, total):
            part = shallow[rows, aligned(k * 1024, 1024)].astype(F32)
            return total + jnp.sum(part * part, axis=1, keepdims=True)

        total = lax.fori_loop(0, 8, squares, jnp.zeros((32, 1), F32))
        scale = lax.rsqrt(total / D + norm_eps)

        @pl.loop(0, NP)
        def _(k):
            here = aligned((k * 2 + at.c) * BLK, BLK)
            there = aligned((k * 2 + at.o) * BLK, BLK)
            nrows = aligned(at.c * ROWS + step * 32, 32)
            nbuf[k, nrows, :] = (shallow[rows, here].astype(F32) * scale * gain[:, here]).astype(BF16)
            pbuf[k, rows, :] = (shallow[rows, there].astype(F32) * scale * gain[:, there]).astype(BF16)

    normed_copy = remote(pbuf, nbuf.at[:, mine], n_send.at[0], n_recv.at[0], peer)
    normed_copy.start()

    group_rows = tbuf.at[at.dp, aligned(at.pipe * 32, 32)]

    def block_copy(k):
        dx, flip, other = GROUP[k]
        slot = at.slot_of("dp", dx, flip)
        if other:
            source = pbuf.at[slot, aligned(at.pipe * 32, 32)]
        else:
            source = nbuf.at[slot, aligned(at.c * ROWS + at.pipe * 32, 32)]
        return remote(source, group_rows, x_send.at[k], x_recv.at[k], at.cross(dx, flip, other))

    def block_arrival(k):
        dx, flip, other = GROUP[k]
        source = at.slot_of("dp", -dx, flip) * 2 + (at.o if other else at.c)
        region = tbuf.at[source, aligned(at.pipe * 32, 32)]
        return remote(region, region, x_send.at[k], x_recv.at[k], peer)

    for k in range(len(GROUP)):
        block_copy(k).start()
    own_block_copy = pltpu.make_async_copy(
        nbuf.at[at.slot, aligned(at.c * ROWS + at.pipe * 32, 32)], group_rows, local_sems.at[3]
    )
    own_block_copy.start()

    wg.middle()
    landed = nbuf.at[:, theirs]
    remote(landed, landed, n_send.at[0], n_recv.at[0], peer).wait_recv()
    own_block_copy.wait()
    for k in range(len(GROUP)):
        block_arrival(k).wait_recv()
    ng.begin()
    wg.late()

    @pl.when(at.swaps)
    def _():
        remote(wo, obuf.at[at.slot], swap_send.at[0], swap_recv.at[0], at.swap()).wait_recv()
        swap.wait_send()

    @pl.when(jnp.logical_not(at.swaps))
    def _():
        keep.wait()

    og.begin()
    wg.finish()

    acc[...] = jnp.zeros_like(acc)

    @pl.loop(0, NP)
    def _(k):
        acc[...] += jnp.dot(nbuf[k], wbuf[k], preferred_element_type=F32)

    sum_mine[...] = acc[theirs, :]
    sums = remote(sum_mine, sum_theirs, n_send.at[1], n_recv.at[1], peer)
    sums.start()
    ng.middle()
    sums.wait_recv()

    cos_table, sin_table = cosine[...], sine[...]
    for head in range(heads):
        cols = pl.ds(head * HD, HD)
        v = acc[mine, cols] + sum_theirs[:, cols]
        qbuf[head] = turned(v, cos_table, sin_table).astype(BF16)
    cols = pl.ds(BLK, HD)
    v = acc[mine, cols] + sum_theirs[:, cols]
    kvbuf[at.pipe] = (turned(v, cos_table, sin_table) * is_key + v * (1.0 - is_key)).astype(BF16)

    def kv_copy(dj):
        region = kvbuf.at[at.pipe]
        return remote(region, region, k_send.at[dj], k_recv.at[dj], at.column(dj, 0))

    def kv_arrival(dj):
        region = kvbuf.at[(at.pipe - dj + NP) % NP]
        return remote(region, region, k_send.at[dj], k_recv.at[dj], peer)

    for dj in range(1, NP):
        kv_copy(dj).start()
    og.middle()
    for dj in range(1, NP):
        kv_arrival(dj).wait_recv()

    score_scale = 1.0 / math.sqrt(HD)
    row_ids = lax.broadcasted_iota(jnp.int32, (ROWS, ROWS), 0)
    col_ids = lax.broadcasted_iota(jnp.int32, (ROWS, ROWS), 1)
    allowed = (seg_column[...] == seg_row[...]) & (col_ids <= row_ids)
    for head in range(heads):
        scores = nt(qbuf[head], kvbuf[2 * head]) * score_scale
        scores = jnp.where(allowed, scores, mask_fill)
        weights = jnp.exp(scores - jnp.max(scores, axis=1, keepdims=True))
        soft = weights * (1.0 / jnp.sum(weights, axis=1, keepdims=True))
        probs[head] = soft
        attended = jnp.dot(soft.astype(BF16), kvbuf[2 * head + 1], preferred_element_type=F32)
        abuf[at.pipe, mine, pl.ds(head * HD, HD)] = attended.astype(BF16)

    def forward(dx, flip):
        k = dx % NX * 2 + flip
        region = abuf.at[at.slot_of("pipe", dx, flip), mine]
        return remote(region, region, f_send.at[k], f_recv.at[k], peer)

    def multiply(dx, flip):
        k = dx % NX * 2 + flip
        source = at.slot_of("pipe", dx, flip)
        region = abuf.at[source, theirs]
        remote(region, region, f_send.at[k], f_recv.at[k], peer).wait_recv()
        acc[:, pl.ds(0, BLK)] += jnp.dot(abuf[source], obuf[source], preferred_element_type=F32)

    ag.begin()
    forward(0, 0).start()
    og.late()
    ng.late()
    ag.middle()
    forward(0, 1).start()
    forward(1, 0).start()
    forward(-1, 0).start()
    ag.late()
    forward(1, 1).start()
    forward(-1, 1).start()
    og.finish()
    acc[...] = jnp.zeros_like(acc)
    for d in ((0, 0), (0, 1), (1, 0), (-1, 0), (1, 1), (-1, 1)):
        multiply(*d)
    ag.wait("a_fp", "a_fm")
    forward(2, 0).start()
    ag.wait("az_fp", "az_fm")
    forward(2, 1).start()
    multiply(2, 0)
    multiply(2, 1)

    own_rows.wait()
    landed = sbuf.at[theirs]
    remote(landed, landed, h_send.at[8], h_recv.at[8], peer).wait_recv()
    own_target.wait()
    for k in range(len(COLUMN)):
        target_arrival(k).wait_recv()

    def wanted_rows(step):
        return target[step // 8, step % 8].astype(F32)

    lane = lax.broadcasted_iota(jnp.int32, (32, 128), 1)

    @pl.loop(0, 2 * NP)
    def _(step):
        rows = aligned(step * 32, 32)
        output = acc[rows, pl.ds(0, BLK)] + sbuf[rows, :].astype(F32)
        acc[rows, pl.ds(0, BLK)] = output
        wanted = wanted_rows(step)
        oo = jnp.sum(output * output, axis=1, keepdims=True)
        tt = jnp.sum(wanted * wanted, axis=1, keepdims=True)
        ot = jnp.sum(output * wanted, axis=1, keepdims=True)
        lanes[rows, :] = jnp.where(
            lane == 0, oo, jnp.where(lane == 1, tt, jnp.where(lane == 2, ot, 0.0))
        )

    square[...] = lanes[...].T
    stat_send[...] = square[pl.ds(0, 8), :]

    def stat(k):
        return remote(
            stat_send, stat_recv.at[k], s_send.at[k], s_recv.at[k], at.column(*COLUMN[k])
        )

    for k in range(len(COLUMN)):
        stat(k).start()
    ng.finish()
    total = stat_send[...]
    for k in range(len(COLUMN)):
        stat(k).wait_recv()
        total = total + stat_recv[k]
    square[pl.ds(0, 8), :] = total
    lanes[...] = square[...].T

    def gradient(step, lost):
        rows = aligned(step * 32, 32)
        output = acc[rows, pl.ds(0, BLK)]
        wanted = wanted_rows(step)
        norm_out = jnp.sqrt(lanes[rows, 0:1] + cosine_eps)
        norm_tar = jnp.sqrt(lanes[rows, 1:2] + cosine_eps)
        both = norm_out * norm_tar
        cosine_sim = lanes[rows, 2:3] / both
        grad = wanted * (1.0 / both) - output * (cosine_sim / (norm_out * norm_out))
        ogbuf[rows, :] = (grad * (-1.0 / 4096)).astype(BF16)
        return lost + (1.0 - cosine_sim)

    lost = lax.fori_loop(0, 2 * NP, gradient, jnp.zeros((32, 1), F32))
    lost = jnp.broadcast_to(jnp.sum(lost, axis=0, keepdims=True), (8, 128))

    grads = Reduce(at, "pipe", g_terms, ROWS, g_corner, g_near, g_cross, None, r_send, r_recv)
    outs = Reduce(at, "dp", o_terms, BLK, o_corner, o_near, o_cross, o_cross_b, e_send, e_recv)
    order = [(2, 1), (2, 0), (1, 1), (-1, 1), (1, 0), (-1, 0), (0, 1), (0, 0)]

    def part(k):
        return remote(part_send.at[k], part_recv.at[k], p_send.at[k], p_recv.at[k], peer)

    def produce(k):
        slot = at.slot_of("pipe", *order[k])
        weights = obuf[slot]
        part_send[k] = nt(ogbuf[theirs, :], weights).astype(BF16)
        part(k).start()
        g_terms[slot] = nt(ogbuf[mine, :], weights).astype(BF16)

    def settle(k):
        part(k).wait_recv()
        grads.add(*order[k], 0, ROWS, part_recv.at[k])

    produce(0)
    produce(1)
    settle(0)
    grads.x_begin(1)
    produce(2)
    settle(1)
    grads.x_begin(0)
    produce(3)
    settle(2)
    produce(4)
    settle(3)
    grads.x_pass(1)
    produce(5)
    settle(4)
    produce(6)
    settle(5)
    grads.x_pass(0)
    produce(7)
    settle(6)
    settle(7)

    @pl.loop(0, NP)
    def _(k):
        o_terms[k] = tn(abuf[k], ogbuf[...]).astype(BF16)

    outs.begin()
    grads.x_end(1)
    grads.z_first()
    grads.x_end(0)
    grads.z_first_add()

    def kv_grad_copy(dj):
        return remote(
            kv_part.at[(at.pipe + dj) % NP], kv_recv.at[dj], d_send.at[dj], d_recv.at[dj],
            at.column(dj, 0),
        )

    for head in range(heads):
        cols = pl.ds(head * HD, HD)
        soft = probs[head]
        att_grad = g_terms[at.pipe, :, cols]
        inner = nt(att_grad, kvbuf[2 * head + 1])
        centred = inner - jnp.sum(soft * inner, axis=1, keepdims=True)
        score_grad = (soft * centred * score_scale).astype(BF16)
        kv_part[2 * head] = tn(score_grad, qbuf[head]).astype(BF16)
        kv_part[2 * head + 1] = tn(soft.astype(BF16), att_grad).astype(BF16)
        grad = jnp.dot(score_grad, kvbuf[2 * head], preferred_element_type=F32)
        qgbuf[at.slot, mine, cols] = turned(grad, cos_table, -sin_table).astype(BF16)

    for dj in range(1, NP):
        kv_grad_copy(dj).start()
    outs.middle()
    total = kv_part[at.pipe].astype(F32)
    for dj in range(1, NP):
        kv_grad_copy(dj).wait_recv()
        total = total + kv_recv[dj].astype(F32)
    total = turned(total, cos_table, -sin_table) * is_key + total * (1.0 - is_key)
    qgbuf[at.slot, mine, pl.ds(BLK, HD)] = total.astype(BF16)

    def hand(dx, flip):
        k = dx % NX * 2 + flip
        region = qgbuf.at[at.slot_of("dp", dx, flip), mine]
        return remote(region, region, h_send.at[k], h_recv.at[k], peer)

    def contract(dx, flip):
        k = dx % NX * 2 + flip
        slot = at.slot_of("dp", dx, flip)
        region = qgbuf.at[slot, theirs]
        remote(region, region, h_send.at[k], h_recv.at[k], peer).wait_recv()
        for core in range(2):
            acc[...] += tn(tbuf[slot * 2 + core], qgbuf[slot, pl.ds(core * ROWS, ROWS), :])

    qg.begin()
    hand(0, 0).start()
    outs.late()
    outs.finish()

    own = at.slot
    give = remote(o_terms.at[own], go_out, swap_send.at[1], swap_recv.at[1], at.swap())
    hold = pltpu.make_async_copy(o_terms.at[own], go_out, local_sems.at[4])

    @pl.when(at.swaps)
    def _():
        give.start()

    @pl.when(jnp.logical_not(at.swaps))
    def _():
        hold.start()

    qg.middle()
    hand(1, 0).start()
    hand(-1, 0).start()
    qg.late()
    acc[...] = jnp.zeros_like(acc)
    contract(0, 0)
    tile = squares_of(lambda rows: o_terms[own, rows, :], BLK, BLK)
    qg.wait("a_fp", "a_fm")
    hand(2, 0).start()
    qg.wait("b_z0")
    hand(0, 1).start()
    contract(1, 0)
    contract(-1, 0)
    qg.wait("b_zm", "b_zp")
    hand(1, 1).start()
    hand(-1, 1).start()
    contract(2, 0)
    contract(0, 1)
    qg.wait("az_fp", "az_fm", "b_z2a", "b_z2b")
    hand(2, 1).start()
    contract(1, 1)
    contract(-1, 1)
    contract(2, 1)
    gq_out[...] = acc[...]
    stat_one[pl.ds(0, 8), :] = tile + squares_of(lambda rows: acc[rows, :], BLK, WQ)
    stat_one[pl.ds(8, 8), :] = lost

    def column_copy(k):
        return remote(
            stat_one, from_column.at[k], c_send.at[k], c_recv.at[k], at.column(*COLUMN[k])
        )

    def plane_copy(k):
        return remote(
            stat_two, from_plane.at[k], l_send.at[k], l_recv.at[k], at.near("dp", *PLANES[k])
        )

    for k in range(len(COLUMN)):
        column_copy(k).start()
    total = stat_one[...]
    for k in range(len(COLUMN)):
        column_copy(k).wait_recv()
        total = total + from_column[k]
    stat_two[...] = total
    for k in range(len(PLANES)):
        plane_copy(k).start()
    for k in range(len(PLANES)):
        plane_copy(k).wait_recv()
        total = total + from_plane[k]
    stat_out[...] = total

    @pl.when(at.swaps)
    def _():
        give.wait_recv()
        give.wait_send()

    @pl.when(jnp.logical_not(at.swaps))
    def _():
        hold.wait()

    for group in (wg, og, ng, ag, qg, grads, outs):
        group.drain()
    normed_copy.wait_send()
    peer_rows.wait_send()
    sums.wait_send()
    for k in range(len(GROUP)):
        block_copy(k).wait_send()
    for k in range(len(COLUMN)):
        target_copy(k).wait_send()
        stat(k).wait_send()
        column_copy(k).wait_send()
    for k in range(len(PLANES)):
        plane_copy(k).wait_send()
    for dj in range(1, NP):
        kv_copy(dj).wait_send()
        kv_grad_copy(dj).wait_send()
    for dx in range(NX):
        for flip in range(2):
            forward(dx, flip).wait_send()
            hand(dx, flip).wait_send()
            part(dx * 2 + flip).wait_send()


def run_step(shallow, gain, wq, wkv, wo, teacher, cosine, sine, seg_column, seg_row):
    vmem = pl.BlockSpec(memory_space=pltpu.VMEM)
    anyspace = pl.BlockSpec(memory_space=pl.ANY)

    def low(*shape):
        return pltpu.VMEM(shape, BF16)

    def wide(*shape):
        return pltpu.VMEM(shape, F32)

    def sems(*counts):
        return [pltpu.SemaphoreType.DMA((count,)) for count in counts for _ in range(2)]

    def reduce_buffers(numbers, half, width):
        return [
            low(numbers, 2, half // 2, width), low(numbers, 2, half, width), low(half, width)
        ]

    return pl.pallas_call(
        step_kernel,
        out_shape=(
            jax.ShapeDtypeStruct((BLK, WQ), F32),
            jax.ShapeDtypeStruct((BLK, BLK), BF16),
            jax.ShapeDtypeStruct((16, 128), F32),
        ),
        in_specs=[vmem, vmem, vmem, vmem, anyspace, anyspace, vmem, vmem, vmem, vmem],
        out_specs=(vmem, vmem, vmem),
        scratch_shapes=[
            low(NP, BLK, WQ), low(NP, BLK, BLK), low(NP, 2 * ROWS, BLK), low(NP, ROWS, BLK),
            low(16, ROWS, BLK), low(2, NP, ROWS // NP, BLK),
            wide(2 * ROWS, WQ), wide(ROWS, WQ), wide(ROWS, WQ),
            low(BLK // HD, ROWS, HD), low(NP, ROWS, HD), wide(BLK // HD, ROWS, ROWS),
            low(NP, 2 * ROWS, BLK), low(2 * ROWS, BLK), low(2 * ROWS, BLK),
            wide(2 * ROWS, 128), wide(128, 2 * ROWS), wide(8, 2 * ROWS), wide(15, 8, 2 * ROWS),
            low(NP, ROWS, BLK), low(NP, ROWS, BLK), low(NP, ROWS, BLK),
            *reduce_buffers(2, ROWS, BLK),
            low(NP, ROWS, HD), low(NP, ROWS, HD),
            low(NP, BLK, BLK), *reduce_buffers(3, BLK // 2, BLK), low(NX, BLK // 2, BLK),
            low(NP, 2 * ROWS, WQ),
            wide(16, 128), wide(16, 128), wide(15, 16, 128), wide(7, 16, 128),
            *sems(
                N_GATHER, N_GATHER, 2, 15, N_FIRST, 15, NP, 2, N_FIRST, NP, 15, NP,
                N_REDUCE_FIRST, NP, N_REDUCE, N_GATHER, NP + 1, 15, 7,
            ),
            pltpu.SemaphoreType.DMA((5,)),
        ],
        compiler_params=pltpu.CompilerParams(
            collective_id=0, has_side_effects=True, vmem_limit_bytes=VLIM
        ),
        name="adapter_step",
    )(shallow, gain, wq, wkv, wo, teacher, cosine, sine, seg_column, seg_row)


def rotary_tables(positions):
    half_width = HD // 2
    exponent = jnp.arange(half_width).astype(F32) * (2.0 / HD)
    inverse = jnp.power(jnp.float32(theta_base), -exponent)
    angle_table = positions.astype(F32)[:, None] * inverse[None, :]
    cosine, sine = jnp.cos(angle_table), jnp.sin(angle_table)
    return jnp.concatenate([cosine, cosine], axis=1), jnp.concatenate([-sine, sine], axis=1)


def per_device(shallow, teacher, positions, segments, in_gain, w_query, w_keyval, w_output):
    all_rows = ROWS * lax.axis_size("dp")
    param_count = D * (2 * QH * HD + 2 * KV * HD)
    cosine, sine = rotary_tables(positions)
    grad_qkv, grad_output, stats = run_step(
        shallow, in_gain[None], w_query, w_keyval, w_output, teacher, cosine, sine,
        segments[:, None], segments[None, :],
    )
    square_total = jnp.sum(stats[:8])
    inverse = 1.0 / jnp.sqrt(square_total / param_count + mean_eps)
    loss_total = stats[8, 0] / lax.axis_size("pipe") / 2
    return (
        loss_total / all_rows,
        grad_qkv[:, :BLK] * inverse,
        grad_qkv[:, BLK:] * inverse,
        grad_output.astype(F32) * inverse,
    )


def solution(mesh):
    placed = (
        P("dp", None),
        P(("dp", "pipe"), None),
        P("dp"),
        P("dp"),
        P(),
        P("dp", "pipe"),
        P("dp", "pipe"),
        P("pipe", "dp"),
    )
    return jax.shard_map(
        per_device,
        mesh=mesh,
        in_specs=placed,
        out_specs=(P(), P("dp", "pipe"), P("dp", "pipe"), P("pipe", "dp")),
        check_vma=False,
    )
```

time: 726 us -> 287 us (0.40)
  waiting for transfers between devices: 525 us -> 0 us
  Pallas kernels: 0 us -> 273 us
  blocking collectives: 94 us -> 0 us
  matrix products: 46.8 us -> 0 us
  other arithmetic: 31.7 us -> 8.48 us
  between operations: 18.8 us -> 3.14 us
    reduce_scatter x3 -> x0, waiting for transfers between devices: 331 us -> none  [the longest x1 203 us: per_device(): lax.psum_scatter(jnp.concatenate([contract_rows(columns, grad_inputs), co...]
    pallas_call x0 -> x1, Pallas kernels: none -> 273 us  [run_step(): pl.pallas_call(step_kernel, out_shape=(jax.ShapeDtypeStruct((BLK, WQ), F3...]
    all_gather x4 -> x0, waiting for transfers between devices: 176 us -> none  [the longest x1 71 us: per_device(): grad_all = lax.all_gather(out_grad, 'pipe', axis=0, tiled=True)]
    psum x1 -> x0, blocking collectives: 64.6 us -> none  [per_device(): loss_total = lax.psum(loss_local, ('dp', 'pipe'))]
    dot_general x13 -> x0, matrix products: 46.2 us -> none  [the longest x2 13.7 us: contract_rows(): lax.dot_general(left, right, (((0,), (0,)), ((), ())), preferred_element_...]
    all_gather x1 -> x0, blocking collectives: 29.5 us -> none  [per_device(): lax.all_gather(keyval_local.reshape(group_rows, keyval_cols), 'pipe', axi...]
    ppermute x1 -> x0, waiting for transfers between devices: 15.5 us -> none  [shifted(): return lax.ppermute(value, axis, pairs)]
    concatenate x4 -> x1, other arithmetic: 14.6 us -> 0.84 us  [rotary_tables(): jnp.concatenate([cosine, cosine], axis=1)]
  transfers between devices with their start and end apart: 8 -> 0, of which waited for: 8 -> 0; matrix products, arithmetic and copies ran while one was open for 4% -> 0% of each run, Pallas kernels for 0% -> 0%
where the time goes in v2:
time: 287 us
  Pallas kernels  273 us (95%)
  other arithmetic  8.48 us (3%)
  between operations  3.14 us (1%)
    pallas_call x1, Pallas kernels, run_step(): pl.pallas_call(step_kernel, out_shape=(jax.ShapeDtypeStruct((BLK, WQ), F3...  273 us

profile of v2, /device:TPU:1, one launch (start us, length us, event | category | flops | bytes accessed | tf_op | source)
XLA Modules:
  0.0 286.9 jit_solution(12749363939402039787)
XLA Ops:
  0.6 0.7 convert_element_type.13
  1.3 1.5 copy.12.seg_column
  2.8 0.5 fusion
  3.3 0.8 pad_maximum_fusion
  4.2 272.6 %adapter_step.1 = (f32[512,640]{1,0:T(8,128)}, bf16[512,512]{1,0:T(8,128)(2,1)}, f32[16,128]{1,0:T(8,128)}) custom-call(bf16[256,8192]{1,0:T(8,128)(2,1)} %shallow.1, f32[1,8192]{1,0:T(1,128)} %bitcast.4, bf16[512,512]{1,0:T(8,128)(2,1)} %wq.1, bf16[512,128]{1,0:T(8,128)(2,1)} %wkv.1, bf16[512,512]{1,0:T(8,128)(2,1)} %wo.1, bf16[32,8192]{1,0:T(8,128)(2,1)} %teacher.1, ...), custom_call_target="tpu_custom_call" | custom-call | tf_op jit(solution)/shard_map/adapter_step/pallas_call | solution.py:834
  276.8 1.3 slice_reduce_fusion
  278.8 1.2 slice.12
  280.6 0.0 copy-start
  280.6 1.7 slice_multiply_fusion.1
  282.4 2.3 slice_multiply_fusion
  284.7 0.0 copy-done
  284.7 1.1 convert_multiply_fusion
  (1 shorter events, 0.0 us)
Async XLA Ops:
  280.6 4.0 %copy-start = (bf16[512,512]{1,0:T(8,128)(2,1)S(1)}, bf16[512,512]{1,0:T(8,128)(2,1)}, u32[]{:S(2)}) copy-start(bf16[512,512]{1,0:T(8,128)(2,1)} %get-tuple-element.9) | copy-start | bytes 1572868

commit v3 on v2

--- a/solution.py
+++ b/solution.py
@@ -17,6 +17,7 @@
 BLK = 512
 ROWS = 256
 WQ = 640
+PARAMS = D * (2 * QH * HD + 2 * KV * HD)
 
 theta_base = 10000.0
 norm_eps = 1e-05
@@ -154,10 +155,12 @@
     def begin(self):
         self.start("a_z", "a_xp", "a_xm")
         if self.halves:
-            self.start("b_xp", "b_xm", "b_z0")
+            self.start("b_xp", "b_xm")
 
     def middle(self):
         self.wait("a_z")
+        if self.halves:
+            self.start("b_z0")
         self.start("az_xp", "az_xm")
         self.wait("a_xp")
         self.start("a_fp")
@@ -338,14 +341,14 @@
 
 
 def step_kernel(
-    shallow, gain, wq, wkv, wo, teacher, cosine, sine, seg_column, seg_row,
-    gq_out, go_out, stat_out,
+    shallow, gain, wq, wkv, wo, teacher, cosine, sine, seg_row,
+    gq_out, gkv_out, go_out, loss_out,
     wbuf, obuf, nbuf, pbuf, tbuf, target, acc, sum_mine, sum_theirs, qbuf, kvbuf, probs,
     abuf, sbuf, ogbuf, lanes, square, stat_send, stat_recv,
     part_send, part_recv, g_terms, g_corner, g_near, g_cross,
     kv_part, kv_recv, o_terms, o_corner, o_near, o_cross, o_cross_b,
-    qgbuf, stat_one, stat_two, from_column, from_plane,
-    w_send, w_recv, o_send, o_recv, n_send, n_recv, x_send, x_recv, m_send, m_recv,
+    qgbuf, go_recv, stat_one, stat_two, from_column, from_plane,
+    w_send, w_recv, v_send, v_recv, o_send, o_recv, n_send, n_recv, x_send, x_recv, m_send, m_recv,
     t_send, t_recv, k_send, k_recv, swap_send, swap_recv,
     a_send, a_recv, f_send, f_recv, s_send, s_recv, p_send, p_recv, r_send, r_recv,
     d_send, d_recv, e_send, e_recv, q_send, q_recv, h_send, h_recv,
@@ -365,7 +368,11 @@
     def slots_mine(buf):
         return lambda slot, row, rows: buf.at[slot, aligned(at.c * ROWS + row, rows)]
 
-    wg = Gather(at, "dp", slots(wbuf), BLK, w_send, w_recv, True)
+    def columns(buf, first, width):
+        return lambda slot, row, rows: buf.at[slot, pl.ds(row, rows), pl.ds(first, width)]
+
+    wg = Gather(at, "dp", columns(wbuf, 0, 384), BLK, w_send, w_recv, True)
+    vg = Gather(at, "dp", columns(wbuf, 384, 256), BLK, v_send, v_recv, True)
     og = Gather(at, "dp", slots(obuf), BLK, o_send, o_recv, True)
     ng = Gather(
         at, "pipe", lambda slot, row, rows: tbuf.at[pl.ds(row, rows), aligned(slot * 32, 32)],
@@ -377,17 +384,10 @@
     wbuf[at.slot, :, pl.ds(0, BLK)] = wq[...]
     wbuf[at.slot, :, pl.ds(BLK, HD)] = wkv[...]
     wg.begin()
+    vg.begin()
 
     swap = remote(wo, obuf.at[at.pipe], swap_send.at[0], swap_recv.at[0], at.swap())
     keep = pltpu.make_async_copy(wo, obuf.at[at.pipe], local_sems.at[0])
-
-    @pl.when(at.swaps)
-    def _():
-        swap.start()
-
-    @pl.when(jnp.logical_not(at.swaps))
-    def _():
-        keep.start()
 
     def target_copy(k):
         dj, other = COLUMN[k]
@@ -403,8 +403,6 @@
         region = target.at[at.o if other else at.c, (at.pipe - dj + NP + 1) % NP]
         return remote(region, region, t_send.at[k], t_recv.at[k], peer)
 
-    for k in range(len(COLUMN)):
-        target_copy(k).start()
     own_block = aligned((at.pipe * 2 + at.c) * BLK, BLK)
     peer_block = aligned((at.pipe * 2 + at.o) * BLK, BLK)
     own_target = pltpu.make_async_copy(
@@ -455,21 +453,21 @@
         region = tbuf.at[source, aligned(at.pipe * 32, 32)]
         return remote(region, region, x_send.at[k], x_recv.at[k], peer)
 
-    for k in range(len(GROUP)):
-        block_copy(k).start()
-    own_block_copy = pltpu.make_async_copy(
-        nbuf.at[at.slot, aligned(at.c * ROWS + at.pipe * 32, 32)], group_rows, local_sems.at[3]
-    )
-    own_block_copy.start()
-
     wg.middle()
+    vg.middle()
+
+    @pl.when(at.swaps)
+    def _():
+        swap.start()
+
+    @pl.when(jnp.logical_not(at.swaps))
+    def _():
+        keep.start()
+
     landed = nbuf.at[:, theirs]
     remote(landed, landed, n_send.at[0], n_recv.at[0], peer).wait_recv()
-    own_block_copy.wait()
-    for k in range(len(GROUP)):
-        block_arrival(k).wait_recv()
-    ng.begin()
     wg.late()
+    vg.late()
 
     @pl.when(at.swaps)
     def _():
@@ -481,18 +479,32 @@
         keep.wait()
 
     og.begin()
-    wg.finish()
+
+    def project(dx, flip):
+        slot = at.slot_of("dp", dx, flip)
+        acc[...] += jnp.dot(nbuf[slot], wbuf[slot], preferred_element_type=F32)
 
     acc[...] = jnp.zeros_like(acc)
-
-    @pl.loop(0, NP)
-    def _(k):
-        acc[...] += jnp.dot(nbuf[k], wbuf[k], preferred_element_type=F32)
+    project(0, 0)
+    project(1, 0)
+    project(-1, 0)
+    wg.wait("b_z0")
+    vg.wait("b_z0")
+    project(0, 1)
+    wg.wait("a_fp", "a_fm")
+    vg.wait("a_fp", "a_fm")
+    project(2, 0)
+    wg.wait("b_zm", "b_zp")
+    vg.wait("b_zm", "b_zp")
+    project(1, 1)
+    project(-1, 1)
+    wg.wait("az_fp", "az_fm", "b_z2a", "b_z2b")
+    vg.wait("az_fp", "az_fm", "b_z2a", "b_z2b")
+    project(2, 1)
 
     sum_mine[...] = acc[theirs, :]
     sums = remote(sum_mine, sum_theirs, n_send.at[1], n_recv.at[1], peer)
     sums.start()
-    ng.middle()
     sums.wait_recv()
 
     cos_table, sin_table = cosine[...], sine[...]
@@ -514,6 +526,8 @@
 
     for dj in range(1, NP):
         kv_copy(dj).start()
+    for k in range(len(COLUMN)):
+        target_copy(k).start()
     og.middle()
     for dj in range(1, NP):
         kv_arrival(dj).wait_recv()
@@ -521,7 +535,8 @@
     score_scale = 1.0 / math.sqrt(HD)
     row_ids = lax.broadcasted_iota(jnp.int32, (ROWS, ROWS), 0)
     col_ids = lax.broadcasted_iota(jnp.int32, (ROWS, ROWS), 1)
-    allowed = (seg_column[...] == seg_row[...]) & (col_ids <= row_ids)
+    ids = jnp.broadcast_to(seg_row[...].astype(F32), (ROWS, ROWS))
+    allowed = (ids.T == ids) & (col_ids <= row_ids)
     for head in range(heads):
         scores = nt(qbuf[head], kvbuf[2 * head]) * score_scale
         scores = jnp.where(allowed, scores, mask_fill)
@@ -546,7 +561,6 @@
     ag.begin()
     forward(0, 0).start()
     og.late()
-    ng.late()
     ag.middle()
     forward(0, 1).start()
     forward(1, 0).start()
@@ -555,6 +569,12 @@
     forward(1, 1).start()
     forward(-1, 1).start()
     og.finish()
+    for k in range(len(GROUP)):
+        block_copy(k).start()
+    own_block_copy = pltpu.make_async_copy(
+        nbuf.at[at.slot, aligned(at.c * ROWS + at.pipe * 32, 32)], group_rows, local_sems.at[3]
+    )
+    own_block_copy.start()
     acc[...] = jnp.zeros_like(acc)
     for d in ((0, 0), (0, 1), (1, 0), (-1, 0), (1, 1), (-1, 1)):
         multiply(*d)
@@ -563,6 +583,10 @@
     ag.wait("az_fp", "az_fm")
     forward(2, 1).start()
     multiply(2, 0)
+    own_block_copy.wait()
+    for k in range(len(GROUP)):
+        block_arrival(k).wait_recv()
+    ng.begin()
     multiply(2, 1)
 
     own_rows.wait()
@@ -600,7 +624,6 @@
 
     for k in range(len(COLUMN)):
         stat(k).start()
-    ng.finish()
     total = stat_send[...]
     for k in range(len(COLUMN)):
         stat(k).wait_recv()
@@ -662,15 +685,24 @@
     settle(6)
     settle(7)
 
-    @pl.loop(0, NP)
-    def _(k):
-        o_terms[k] = tn(abuf[k], ogbuf[...]).astype(BF16)
-
-    outs.begin()
+    def out_term(dx, flip):
+        slot = at.slot_of("dp", dx, flip)
+        o_terms[slot] = tn(abuf[slot], ogbuf[...]).astype(BF16)
+
+    out_term(2, 1)
     grads.x_end(1)
     grads.z_first()
+    out_term(2, 0)
+    outs.x_begin(1)
+    outs.x_begin(0)
+    out_term(1, 1)
     grads.x_end(0)
+    out_term(3, 1)
+    out_term(0, 1)
     grads.z_first_add()
+    for dx in (2, 1, 3, 0):
+        outs.z_second(dx)
+    ng.middle()
 
     def kv_grad_copy(dj):
         return remote(
@@ -692,7 +724,12 @@
 
     for dj in range(1, NP):
         kv_grad_copy(dj).start()
-    outs.middle()
+    out_term(1, 0)
+    out_term(-1, 0)
+    out_term(0, 0)
+    outs.x_pass(1)
+    outs.z_second_add(2)
+    outs.x_begin(2)
     total = kv_part[at.pipe].astype(F32)
     for dj in range(1, NP):
         kv_grad_copy(dj).wait_recv()
@@ -710,17 +747,27 @@
         slot = at.slot_of("dp", dx, flip)
         region = qgbuf.at[slot, theirs]
         remote(region, region, h_send.at[k], h_recv.at[k], peer).wait_recv()
-        for core in range(2):
-            acc[...] += tn(tbuf[slot * 2 + core], qgbuf[slot, pl.ds(core * ROWS, ROWS), :])
+        acc[...] += jnp.dot(
+            wbuf[slot, :, pl.ds(0, BLK)], qgbuf[slot], preferred_element_type=F32
+        )
 
     qg.begin()
     hand(0, 0).start()
+    outs.x_pass(0)
+    outs.z_second_add(1)
+    outs.z_second_add(3)
+    outs.x_pass(2)
+    ng.late()
+    qg.middle()
+    hand(1, 0).start()
+    hand(-1, 0).start()
     outs.late()
+    qg.late()
     outs.finish()
 
     own = at.slot
-    give = remote(o_terms.at[own], go_out, swap_send.at[1], swap_recv.at[1], at.swap())
-    hold = pltpu.make_async_copy(o_terms.at[own], go_out, local_sems.at[4])
+    give = remote(o_terms.at[own], go_recv, swap_send.at[1], swap_recv.at[1], at.swap())
+    hold = pltpu.make_async_copy(o_terms.at[own], go_recv, local_sems.at[4])
 
     @pl.when(at.swaps)
     def _():
@@ -730,30 +777,34 @@
     def _():
         hold.start()
 
-    qg.middle()
-    hand(1, 0).start()
-    hand(-1, 0).start()
-    qg.late()
+    ng.finish()
+    wg.drain()
+    vg.drain()
+
+    @pl.loop(0, NP)
+    def _(k):
+        for core in range(2):
+            wbuf[k, :, pl.ds(core * ROWS, ROWS)] = tbuf[k * 2 + core].T
+
     acc[...] = jnp.zeros_like(acc)
     contract(0, 0)
-    tile = squares_of(lambda rows: o_terms[own, rows, :], BLK, BLK)
-    qg.wait("a_fp", "a_fm")
-    hand(2, 0).start()
     qg.wait("b_z0")
     hand(0, 1).start()
     contract(1, 0)
     contract(-1, 0)
+    qg.wait("a_fp", "a_fm")
+    hand(2, 0).start()
     qg.wait("b_zm", "b_zp")
     hand(1, 1).start()
     hand(-1, 1).start()
+    contract(0, 1)
     contract(2, 0)
-    contract(0, 1)
+    tile = squares_of(lambda rows: o_terms[own, rows, :], BLK, BLK)
     qg.wait("az_fp", "az_fm", "b_z2a", "b_z2b")
     hand(2, 1).start()
     contract(1, 1)
     contract(-1, 1)
     contract(2, 1)
-    gq_out[...] = acc[...]
     stat_one[pl.ds(0, 8), :] = tile + squares_of(lambda rows: acc[rows, :], BLK, WQ)
     stat_one[pl.ds(8, 8), :] = lost
 
@@ -779,7 +830,13 @@
     for k in range(len(PLANES)):
         plane_copy(k).wait_recv()
         total = total + from_plane[k]
-    stat_out[...] = total
+    square_sum = jnp.sum(
+        jnp.sum(total[:8], axis=0, keepdims=True), axis=1, keepdims=True
+    )
+    inverse = 1.0 / jnp.sqrt(square_sum * (1.0 / PARAMS) + mean_eps)
+    loss_out[...] = total[8:] * (1.0 / (2 * NP * 4096))
+    gq_out[...] = acc[:, pl.ds(0, BLK)] * inverse
+    gkv_out[...] = acc[:, pl.ds(BLK, HD)] * inverse
 
     @pl.when(at.swaps)
     def _():
@@ -790,7 +847,8 @@
     def _():
         hold.wait()
 
-    for group in (wg, og, ng, ag, qg, grads, outs):
+    go_out[...] = go_recv[...].astype(F32) * inverse
+    for group in (og, ng, ag, qg, grads, outs):
         group.drain()
     normed_copy.wait_send()
     peer_rows.wait_send()
@@ -813,7 +871,7 @@
             part(dx * 2 + flip).wait_send()
 
 
-def run_step(shallow, gain, wq, wkv, wo, teacher, cosine, sine, seg_column, seg_row):
+def run_step(shallow, gain, wq, wkv, wo, teacher, cosine, sine, seg_row):
     vmem = pl.BlockSpec(memory_space=pltpu.VMEM)
     anyspace = pl.BlockSpec(memory_space=pl.ANY)
 
@@ -834,12 +892,13 @@
     return pl.pallas_call(
         step_kernel,
         out_shape=(
-            jax.ShapeDtypeStruct((BLK, WQ), F32),
-            jax.ShapeDtypeStruct((BLK, BLK), BF16),
-            jax.ShapeDtypeStruct((16, 128), F32),
+            jax.ShapeDtypeStruct((BLK, BLK), F32),
+            jax.ShapeDtypeStruct((BLK, HD), F32),
+            jax.ShapeDtypeStruct((BLK, BLK), F32),
+            jax.ShapeDtypeStruct((8, 128), F32),
         ),
-        in_specs=[vmem, vmem, vmem, vmem, anyspace, anyspace, vmem, vmem, vmem, vmem],
-        out_specs=(vmem, vmem, vmem),
+        in_specs=[vmem, vmem, vmem, vmem, anyspace, anyspace, vmem, vmem, vmem],
+        out_specs=(vmem, vmem, vmem, vmem),
         scratch_shapes=[
             low(NP, BLK, WQ), low(NP, BLK, BLK), low(NP, 2 * ROWS, BLK), low(NP, ROWS, BLK),
             low(16, ROWS, BLK), low(2, NP, ROWS // NP, BLK),
@@ -851,10 +910,10 @@
             *reduce_buffers(2, ROWS, BLK),
             low(NP, ROWS, HD), low(NP, ROWS, HD),
             low(NP, BLK, BLK), *reduce_buffers(3, BLK // 2, BLK), low(NX, BLK // 2, BLK),
-            low(NP, 2 * ROWS, WQ),
+            low(NP, 2 * ROWS, WQ), low(BLK, BLK),
             wide(16, 128), wide(16, 128), wide(15, 16, 128), wide(7, 16, 128),
             *sems(
-                N_GATHER, N_GATHER, 2, 15, N_FIRST, 15, NP, 2, N_FIRST, NP, 15, NP,
+                N_GATHER, N_GATHER, N_GATHER, 2, 15, N_FIRST, 15, NP, 2, N_FIRST, NP, 15, NP,
                 N_REDUCE_FIRST, NP, N_REDUCE, N_GATHER, NP + 1, 15, 7,
             ),
             pltpu.SemaphoreType.DMA((5,)),
@@ -863,7 +922,7 @@
             collective_id=0, has_side_effects=True, vmem_limit_bytes=VLIM
         ),
         name="adapter_step",
-    )(shallow, gain, wq, wkv, wo, teacher, cosine, sine, seg_column, seg_row)
+    )(shallow, gain, wq, wkv, wo, teacher, cosine, sine, seg_row)
 
 
 def rotary_tables(positions):
@@ -876,22 +935,12 @@
 
 
 def per_device(shallow, teacher, positions, segments, in_gain, w_query, w_keyval, w_output):
-    all_rows = ROWS * lax.axis_size("dp")
-    param_count = D * (2 * QH * HD + 2 * KV * HD)
     cosine, sine = rotary_tables(positions)
-    grad_qkv, grad_output, stats = run_step(
+    step_query, step_keyval, step_output, loss = run_step(
         shallow, in_gain[None], w_query, w_keyval, w_output, teacher, cosine, sine,
-        segments[:, None], segments[None, :],
+        segments[None, :],
     )
-    square_total = jnp.sum(stats[:8])
-    inverse = 1.0 / jnp.sqrt(square_total / param_count + mean_eps)
-    loss_total = stats[8, 0] / lax.axis_size("pipe") / 2
-    return (
-        loss_total / all_rows,
-        grad_qkv[:, :BLK] * inverse,
-        grad_qkv[:, BLK:] * inverse,
-        grad_output.astype(F32) * inverse,
-    )
+    return loss[0, 0], step_query, step_keyval, step_output
 
 
 def solution(mesh):

time: 287 us -> 269 us (0.937)
  Pallas kernels: 273 us -> 258 us
  other arithmetic: 8.48 us -> 2.07 us
  local copies, waits for them, and re-layouts: 2.66 us -> 7.36 us
    pallas_call x1, Pallas kernels: 273 us -> 258 us  [run_step(): pl.pallas_call(step_kernel, out_shape=(jax.ShapeDtypeStruct((BLK, BLK), F...]
    unnamed x2 -> x3, local copies, waits for them, and re-layouts: 0.01 us -> 6.19 us
    mul x3 -> x0, other arithmetic: 5.13 us -> none  [the longest x1 2.28 us: per_device(): grad_qkv[:, :BLK] * inverse]
where the time goes in v3:
time: 269 us; the launch traced here: 268 us
  Pallas kernels  258 us (96%)
  local copies, waits for them, and re-layouts  7.36 us (3%)
    pallas_call x1, Pallas kernels, run_step(): pl.pallas_call(step_kernel, out_shape=(jax.ShapeDtypeStruct((BLK, BLK), F...  258 us
    unnamed x3, local copies, waits for them, and re-layouts  6.19 us

profile of v3, /device:TPU:1, one launch (start us, length us, event | category | flops | bytes accessed | tf_op | source)
XLA Modules:
  0.0 268.4 jit_solution(478784183734578796)
XLA Ops:
  0.6 0.7 convert_element_type.10
  1.3 0.5 fusion
  1.9 0.8 pad_maximum_fusion
  2.7 258.4 %adapter_step.1 = (f32[512,512]{1,0:T(8,128)}, f32[512,128]{1,0:T(8,128)}, f32[512,512]{1,0:T(8,128)}, f32[8,128]{1,0:T(8,128)}) custom-call(bf16[256,8192]{1,0:T(8,128)(2,1)} %shallow.1, f32[1,8192]{1,0:T(1,128)} %bitcast.3, bf16[512,512]{1,0:T(8,128)(2,1)} %wq.1, bf16[512,128]{1,0:T(8,128)(2,1)} %wkv.1, bf16[512,512]{1,0:T(8,128)(2,1)} %wo.1, ...), custom_call_target="tpu_custom_call" | custom-call | tf_op jit(solution)/shard_map/adapter_step/pallas_call | solution.py:892
  261.1 1.2 slice.3
  262.3 2.3 copy.15
  264.5 1.7 copy.16
  266.2 2.3 copy.17
  (1 shorter events, 0.0 us)

commit v4 on v3

--- a/solution.py
+++ b/solution.py
@@ -456,14 +456,6 @@
     wg.middle()
     vg.middle()
 
-    @pl.when(at.swaps)
-    def _():
-        swap.start()
-
-    @pl.when(jnp.logical_not(at.swaps))
-    def _():
-        keep.start()
-
     landed = nbuf.at[:, theirs]
     remote(landed, landed, n_send.at[0], n_recv.at[0], peer).wait_recv()
     wg.late()
@@ -471,14 +463,11 @@
 
     @pl.when(at.swaps)
     def _():
-        remote(wo, obuf.at[at.slot], swap_send.at[0], swap_recv.at[0], at.swap()).wait_recv()
-        swap.wait_send()
+        swap.start()
 
     @pl.when(jnp.logical_not(at.swaps))
     def _():
-        keep.wait()
-
-    og.begin()
+        keep.start()
 
     def project(dx, flip):
         slot = at.slot_of("dp", dx, flip)
@@ -528,7 +517,17 @@
         kv_copy(dj).start()
     for k in range(len(COLUMN)):
         target_copy(k).start()
-    og.middle()
+
+    @pl.when(at.swaps)
+    def _():
+        remote(wo, obuf.at[at.slot], swap_send.at[0], swap_recv.at[0], at.swap()).wait_recv()
+        swap.wait_send()
+
+    @pl.when(jnp.logical_not(at.swaps))
+    def _():
+        keep.wait()
+
+    og.begin()
     for dj in range(1, NP):
         kv_arrival(dj).wait_recv()
 
@@ -560,21 +559,22 @@
 
     ag.begin()
     forward(0, 0).start()
-    og.late()
+    og.middle()
     ag.middle()
     forward(0, 1).start()
     forward(1, 0).start()
     forward(-1, 0).start()
     ag.late()
-    forward(1, 1).start()
-    forward(-1, 1).start()
-    og.finish()
+    og.late()
     for k in range(len(GROUP)):
         block_copy(k).start()
     own_block_copy = pltpu.make_async_copy(
         nbuf.at[at.slot, aligned(at.c * ROWS + at.pipe * 32, 32)], group_rows, local_sems.at[3]
     )
     own_block_copy.start()
+    forward(1, 1).start()
+    forward(-1, 1).start()
+    og.finish()
     acc[...] = jnp.zeros_like(acc)
     for d in ((0, 0), (0, 1), (1, 0), (-1, 0), (1, 1), (-1, 1)):
         multiply(*d)
@@ -583,10 +583,6 @@
     ag.wait("az_fp", "az_fm")
     forward(2, 1).start()
     multiply(2, 0)
-    own_block_copy.wait()
-    for k in range(len(GROUP)):
-        block_arrival(k).wait_recv()
-    ng.begin()
     multiply(2, 1)
 
     own_rows.wait()
@@ -624,6 +620,10 @@
 
     for k in range(len(COLUMN)):
         stat(k).start()
+    own_block_copy.wait()
+    for k in range(len(GROUP)):
+        block_arrival(k).wait_recv()
+    ng.begin()
     total = stat_send[...]
     for k in range(len(COLUMN)):
         stat(k).wait_recv()
@@ -664,17 +664,30 @@
         part(k).wait_recv()
         grads.add(*order[k], 0, ROWS, part_recv.at[k])
 
+    def out_term(dx, flip):
+        slot = at.slot_of("dp", dx, flip)
+        o_terms[slot] = tn(abuf[slot], ogbuf[...]).astype(BF16)
+
+    out_term(2, 1)
+    outs.z_second(2)
+    outs.x_begin(1)
     produce(0)
     produce(1)
     settle(0)
     grads.x_begin(1)
+    out_term(2, 0)
+    outs.x_begin(0)
     produce(2)
     settle(1)
     grads.x_begin(0)
+    out_term(1, 1)
+    outs.z_second(1)
     produce(3)
     settle(2)
     produce(4)
     settle(3)
+    out_term(3, 1)
+    outs.z_second(3)
     grads.x_pass(1)
     produce(5)
     settle(4)
@@ -684,24 +697,16 @@
     produce(7)
     settle(6)
     settle(7)
-
-    def out_term(dx, flip):
-        slot = at.slot_of("dp", dx, flip)
-        o_terms[slot] = tn(abuf[slot], ogbuf[...]).astype(BF16)
-
-    out_term(2, 1)
+    outs.x_pass(1)
     grads.x_end(1)
     grads.z_first()
-    out_term(2, 0)
-    outs.x_begin(1)
-    outs.x_begin(0)
-    out_term(1, 1)
+    out_term(1, 0)
+    out_term(-1, 0)
+    out_term(0, 1)
     grads.x_end(0)
-    out_term(3, 1)
-    out_term(0, 1)
     grads.z_first_add()
-    for dx in (2, 1, 3, 0):
-        outs.z_second(dx)
+    outs.z_second(0)
+    outs.x_pass(0)
     ng.middle()
 
     def kv_grad_copy(dj):
@@ -724,12 +729,11 @@
 
     for dj in range(1, NP):
         kv_grad_copy(dj).start()
-    out_term(1, 0)
-    out_term(-1, 0)
-    out_term(0, 0)
-    outs.x_pass(1)
     outs.z_second_add(2)
     outs.x_begin(2)
+    out_term(0, 0)
+    outs.z_second_add(1)
+    outs.z_second_add(3)
     total = kv_part[at.pipe].astype(F32)
     for dj in range(1, NP):
         kv_grad_copy(dj).wait_recv()
@@ -753,30 +757,10 @@
 
     qg.begin()
     hand(0, 0).start()
-    outs.x_pass(0)
-    outs.z_second_add(1)
-    outs.z_second_add(3)
+    ng.late()
+    outs.x_end(1)
+    outs.z_first()
     outs.x_pass(2)
-    ng.late()
-    qg.middle()
-    hand(1, 0).start()
-    hand(-1, 0).start()
-    outs.late()
-    qg.late()
-    outs.finish()
-
-    own = at.slot
-    give = remote(o_terms.at[own], go_recv, swap_send.at[1], swap_recv.at[1], at.swap())
-    hold = pltpu.make_async_copy(o_terms.at[own], go_recv, local_sems.at[4])
-
-    @pl.when(at.swaps)
-    def _():
-        give.start()
-
-    @pl.when(jnp.logical_not(at.swaps))
-    def _():
-        hold.start()
-
     ng.finish()
     wg.drain()
     vg.drain()
@@ -785,6 +769,25 @@
     def _(k):
         for core in range(2):
             wbuf[k, :, pl.ds(core * ROWS, ROWS)] = tbuf[k * 2 + core].T
+    qg.middle()
+    hand(1, 0).start()
+    hand(-1, 0).start()
+    outs.x_end(0)
+    outs.z_second_add(0)
+    qg.late()
+    outs.finish()
+
+    own = at.slot
+    give = remote(o_terms.at[own], go_recv, swap_send.at[1], swap_recv.at[1], at.swap())
+    hold = pltpu.make_async_copy(o_terms.at[own], go_recv, local_sems.at[4])
+
+    @pl.when(at.swaps)
+    def _():
+        give.start()
+
+    @pl.when(jnp.logical_not(at.swaps))
+    def _():
+        hold.start()
 
     acc[...] = jnp.zeros_like(acc)
     contract(0, 0)

time: 269 us -> 252 us (0.937)
  Pallas kernels: 258 us -> 242 us
    pallas_call x1, Pallas kernels: 258 us -> 242 us  [run_step(): pl.pallas_call(step_kernel, out_shape=(jax.ShapeDtypeStruct((BLK, BLK), F...]
where the time goes in v4:
time: 252 us
  Pallas kernels  242 us (96%)
  local copies, waits for them, and re-layouts  7.36 us (3%)
    pallas_call x1, Pallas kernels, run_step(): pl.pallas_call(step_kernel, out_shape=(jax.ShapeDtypeStruct((BLK, BLK), F...  242 us
    unnamed x3, local copies, waits for them, and re-layouts  6.19 us

profile of v4, /device:TPU:1, one launch (start us, length us, event | category | flops | bytes accessed | tf_op | source)
XLA Modules:
  0.0 252.1 jit_solution(1101671994766334377)
XLA Ops:
  0.6 0.7 convert_element_type.10
  1.3 0.5 fusion
  1.9 0.8 pad_maximum_fusion
  2.7 242.0 %adapter_step.1 = (f32[512,512]{1,0:T(8,128)}, f32[512,128]{1,0:T(8,128)}, f32[512,512]{1,0:T(8,128)}, f32[8,128]{1,0:T(8,128)}) custom-call(bf16[256,8192]{1,0:T(8,128)(2,1)} %shallow.1, f32[1,8192]{1,0:T(1,128)} %bitcast.3, bf16[512,512]{1,0:T(8,128)(2,1)} %wq.1, bf16[512,128]{1,0:T(8,128)(2,1)} %wkv.1, bf16[512,512]{1,0:T(8,128)(2,1)} %wo.1, ...), custom_call_target="tpu_custom_call" | custom-call | tf_op jit(solution)/shard_map/adapter_step/pallas_call | solution.py:895
  244.7 1.2 slice.3
  245.9 2.3 copy.15
  248.2 1.7 copy.16
  249.8 2.3 copy.17
  (1 shorter events, 0.0 us)

commit v5 on v4

--- a/solution.py
+++ b/solution.py
@@ -342,7 +342,7 @@
 
 def step_kernel(
     shallow, gain, wq, wkv, wo, teacher, cosine, sine, seg_row,
-    gq_out, gkv_out, go_out, loss_out,
+    gq_out, gkv_out, go_out, scale_out,
     wbuf, obuf, nbuf, pbuf, tbuf, target, acc, sum_mine, sum_theirs, qbuf, kvbuf, probs,
     abuf, sbuf, ogbuf, lanes, square, stat_send, stat_recv,
     part_send, part_recv, g_terms, g_corner, g_near, g_cross,
@@ -351,7 +351,7 @@
     w_send, w_recv, v_send, v_recv, o_send, o_recv, n_send, n_recv, x_send, x_recv, m_send, m_recv,
     t_send, t_recv, k_send, k_recv, swap_send, swap_recv,
     a_send, a_recv, f_send, f_recv, s_send, s_recv, p_send, p_recv, r_send, r_recv,
-    d_send, d_recv, e_send, e_recv, q_send, q_recv, h_send, h_recv,
+    d_send, d_recv, e_send, e_recv, q_send, q_recv, u_send, u_recv, h_send, h_recv,
     c_send, c_recv, l_send, l_recv, local_sems,
 ):
     at = Place()
@@ -379,7 +379,14 @@
         16, m_send, m_recv, False,
     )
     ag = Gather(at, "pipe", slots_mine(abuf), ROWS, a_send, a_recv, False)
-    qg = Gather(at, "dp", slots_mine(qgbuf), ROWS, q_send, q_recv, True)
+
+    def columns_mine(buf, first, width):
+        return lambda slot, row, rows: buf.at[
+            slot, aligned(at.c * ROWS + row, rows), pl.ds(first, width)
+        ]
+
+    qg = Gather(at, "dp", columns_mine(qgbuf, 0, BLK), ROWS, q_send, q_recv, True)
+    kg = Gather(at, "dp", columns_mine(qgbuf, BLK, HD), ROWS, u_send, u_recv, True)
 
     wbuf[at.slot, :, pl.ds(0, BLK)] = wq[...]
     wbuf[at.slot, :, pl.ds(BLK, HD)] = wkv[...]
@@ -729,6 +736,7 @@
 
     for dj in range(1, NP):
         kv_grad_copy(dj).start()
+    qg.begin()
     outs.z_second_add(2)
     outs.x_begin(2)
     out_term(0, 0)
@@ -755,7 +763,7 @@
             wbuf[slot, :, pl.ds(0, BLK)], qgbuf[slot], preferred_element_type=F32
         )
 
-    qg.begin()
+    kg.begin()
     hand(0, 0).start()
     ng.late()
     outs.x_end(1)
@@ -770,11 +778,13 @@
         for core in range(2):
             wbuf[k, :, pl.ds(core * ROWS, ROWS)] = tbuf[k * 2 + core].T
     qg.middle()
+    kg.middle()
     hand(1, 0).start()
     hand(-1, 0).start()
     outs.x_end(0)
     outs.z_second_add(0)
     qg.late()
+    kg.late()
     outs.finish()
 
     own = at.slot
@@ -792,18 +802,22 @@
     acc[...] = jnp.zeros_like(acc)
     contract(0, 0)
     qg.wait("b_z0")
+    kg.wait("b_z0")
     hand(0, 1).start()
     contract(1, 0)
     contract(-1, 0)
     qg.wait("a_fp", "a_fm")
+    kg.wait("a_fp", "a_fm")
     hand(2, 0).start()
     qg.wait("b_zm", "b_zp")
+    kg.wait("b_zm", "b_zp")
     hand(1, 1).start()
     hand(-1, 1).start()
     contract(0, 1)
     contract(2, 0)
     tile = squares_of(lambda rows: o_terms[own, rows, :], BLK, BLK)
     qg.wait("az_fp", "az_fm", "b_z2a", "b_z2b")
+    kg.wait("az_fp", "az_fm", "b_z2a", "b_z2b")
     hand(2, 1).start()
     contract(1, 1)
     contract(-1, 1)
@@ -823,6 +837,8 @@
 
     for k in range(len(COLUMN)):
         column_copy(k).start()
+    gq_out[...] = acc[:, pl.ds(0, BLK)].astype(BF16)
+    gkv_out[...] = acc[:, pl.ds(BLK, HD)].astype(BF16)
     total = stat_one[...]
     for k in range(len(COLUMN)):
         column_copy(k).wait_recv()
@@ -837,9 +853,8 @@
         jnp.sum(total[:8], axis=0, keepdims=True), axis=1, keepdims=True
     )
     inverse = 1.0 / jnp.sqrt(square_sum * (1.0 / PARAMS) + mean_eps)
-    loss_out[...] = total[8:] * (1.0 / (2 * NP * 4096))
-    gq_out[...] = acc[:, pl.ds(0, BLK)] * inverse
-    gkv_out[...] = acc[:, pl.ds(BLK, HD)] * inverse
+    scale_out[pl.ds(0, 8), :] = jnp.broadcast_to(inverse, (8, 128))
+    scale_out[pl.ds(8, 8), :] = total[8:] * (1.0 / (2 * NP * 4096))
 
     @pl.when(at.swaps)
     def _():
@@ -850,8 +865,8 @@
     def _():
         hold.wait()
 
-    go_out[...] = go_recv[...].astype(F32) * inverse
-    for group in (og, ng, ag, qg, grads, outs):
+    go_out[...] = go_recv[...]
+    for group in (og, ng, ag, qg, kg, grads, outs):
         group.drain()
     normed_copy.wait_send()
     peer_rows.wait_send()
@@ -895,10 +910,10 @@
     return pl.pallas_call(
         step_kernel,
         out_shape=(
-            jax.ShapeDtypeStruct((BLK, BLK), F32),
-            jax.ShapeDtypeStruct((BLK, HD), F32),
-            jax.ShapeDtypeStruct((BLK, BLK), F32),
-            jax.ShapeDtypeStruct((8, 128), F32),
+            jax.ShapeDtypeStruct((BLK, BLK), BF16),
+            jax.ShapeDtypeStruct((BLK, HD), BF16),
+            jax.ShapeDtypeStruct((BLK, BLK), BF16),
+            jax.ShapeDtypeStruct((16, 128), F32),
         ),
         in_specs=[vmem, vmem, vmem, vmem, anyspace, anyspace, vmem, vmem, vmem],
         out_specs=(vmem, vmem, vmem, vmem),
@@ -917,7 +932,7 @@
             wide(16, 128), wide(16, 128), wide(15, 16, 128), wide(7, 16, 128),
             *sems(
                 N_GATHER, N_GATHER, N_GATHER, 2, 15, N_FIRST, 15, NP, 2, N_FIRST, NP, 15, NP,
-                N_REDUCE_FIRST, NP, N_REDUCE, N_GATHER, NP + 1, 15, 7,
+                N_REDUCE_FIRST, NP, N_REDUCE, N_GATHER, N_GATHER, NP + 1, 15, 7,
             ),
             pltpu.SemaphoreType.DMA((5,)),
         ],
@@ -939,11 +954,17 @@
 
 def per_device(shallow, teacher, positions, segments, in_gain, w_query, w_keyval, w_output):
     cosine, sine = rotary_tables(positions)
-    step_query, step_keyval, step_output, loss = run_step(
+    query, keyval, output, scale = run_step(
         shallow, in_gain[None], w_query, w_keyval, w_output, teacher, cosine, sine,
         segments[None, :],
     )
-    return loss[0, 0], step_query, step_keyval, step_output
+    inverse = scale[:1, :1]
+    return (
+        scale[8, 0],
+        query.astype(F32) * inverse,
+        keyval.astype(F32) * inverse,
+        output.astype(F32) * inverse,
+    )
 
 
 def solution(mesh):

time: 252 us -> 250 us (level)
  other arithmetic: 2.07 us -> 10.1 us
  local copies, waits for them, and re-layouts: 7.36 us -> 1.28 us
  Pallas kernels: 242 us -> 237 us
    mul x0 -> x3, other arithmetic: none -> 8 us  [the longest x1 2.84 us: per_device(): output.astype(F32) * inverse]
    unnamed x3 -> x0, local copies, waits for them, and re-layouts: 6.19 us -> none
    pallas_call x1, Pallas kernels: 242 us -> 237 us  [run_step(): pl.pallas_call(step_kernel, out_shape=(jax.ShapeDtypeStruct((BLK, BLK), B...]
where the time goes in v5:
time: 250 us; the launch traced here: 249 us
  Pallas kernels  237 us (95%)
  other arithmetic  10.1 us (4%)
    pallas_call x1, Pallas kernels, run_step(): pl.pallas_call(step_kernel, out_shape=(jax.ShapeDtypeStruct((BLK, BLK), B...  237 us

profile of v5, /device:TPU:1, one launch (start us, length us, event | category | flops | bytes accessed | tf_op | source)
XLA Modules:
  0.0 249.2 jit_solution(17747446766498424531)
XLA Ops:
  0.6 0.7 convert_element_type.19
  1.3 0.5 fusion
  1.9 0.8 pad_maximum_fusion
  2.7 237.2 %adapter_step.1 = (bf16[512,512]{1,0:T(8,128)(2,1)}, bf16[512,128]{1,0:T(8,128)(2,1)}, bf16[512,512]{1,0:T(8,128)(2,1)}, f32[16,128]{1,0:T(8,128)}) custom-call(bf16[256,8192]{1,0:T(8,128)(2,1)} %shallow.1, f32[1,8192]{1,0:T(1,128)} %bitcast.4, bf16[512,512]{1,0:T(8,128)(2,1)} %wq.1, bf16[512,128]{1,0:T(8,128)(2,1)} %wkv.1, bf16[512,512]{1,0:T(8,128)(2,1)} %wo.1, ...), custom_call_target="tpu_custom_call" | custom-call | tf_op jit(solution)/shard_map/adapter_step/pallas_call | solution.py:910
  240.0 1.3 fusion.1
  241.2 2.3 convert_multiply_fusion.2
  243.6 2.8 %convert_multiply_fusion = f32[512,512]{1,0:T(8,128)} fusion(bf16[512,512]{1,0:T(8,128)(2,1)} %get-tuple-element.11, f32[]{:T(128)} %bitcast.3), kind=kLoop, calls=%fused_computation | loop fusion | flops 524288 | bytes 1572868 | tf_op jit(solution)/shard_map/mul | solution.py:966
  246.4 2.8 %convert_multiply_fusion.1 = f32[512,512]{1,0:T(8,128)} fusion(bf16[512,512]{1,0:T(8,128)(2,1)} %get-tuple-element.9, f32[]{:T(128)} %bitcast.3), kind=kLoop, calls=%fused_computation.1 | loop fusion | flops 524288 | bytes 1572868 | tf_op jit(solution)/shard_map/mul | solution.py:964
  (1 shorter events, 0.0 us)

commit v6 on v5

--- a/solution.py
+++ b/solution.py
@@ -958,7 +958,7 @@
         shallow, in_gain[None], w_query, w_keyval, w_output, teacher, cosine, sine,
         segments[None, :],
     )
-    inverse = scale[:1, :1]
+    inverse = scale[0, 0]
     return (
         scale[8, 0],
         query.astype(F32) * inverse,

time: 250 us -> 250 us (level)
  no operation moved by 1% of the time
where the time goes in v6:
time: 250 us; the launch traced here: 249 us
  Pallas kernels  237 us (95%)
  other arithmetic  10.1 us (4%)
    pallas_call x1, Pallas kernels, run_step(): pl.pallas_call(step_kernel, out_shape=(jax.ShapeDtypeStruct((BLK, BLK), B...  237 us

profile of v6, /device:TPU:1, one launch (start us, length us, event | category | flops | bytes accessed | tf_op | source)
XLA Modules:
  0.0 249.2 jit_solution(17747446766498424531)
XLA Ops:
  0.6 0.7 convert_element_type.19
  1.3 0.5 fusion
  1.9 0.8 pad_maximum_fusion
  2.7 237.2 %adapter_step.1 = (bf16[512,512]{1,0:T(8,128)(2,1)}, bf16[512,128]{1,0:T(8,128)(2,1)}, bf16[512,512]{1,0:T(8,128)(2,1)}, f32[16,128]{1,0:T(8,128)}) custom-call(bf16[256,8192]{1,0:T(8,128)(2,1)} %shallow.1, f32[1,8192]{1,0:T(1,128)} %bitcast.4, bf16[512,512]{1,0:T(8,128)(2,1)} %wq.1, bf16[512,128]{1,0:T(8,128)(2,1)} %wkv.1, bf16[512,512]{1,0:T(8,128)(2,1)} %wo.1, ...), custom_call_target="tpu_custom_call" | custom-call | tf_op jit(solution)/shard_map/adapter_step/pallas_call | solution.py:910
  240.0 1.3 fusion.1
  241.2 2.3 convert_multiply_fusion.2
  243.6 2.8 %convert_multiply_fusion = f32[512,512]{1,0:T(8,128)} fusion(bf16[512,512]{1,0:T(8,128)(2,1)} %get-tuple-element.11, f32[]{:T(128)} %bitcast.3), kind=kLoop, calls=%fused_computation | loop fusion | flops 524288 | bytes 1572868 | tf_op jit(solution)/shard_map/mul | solution.py:966
  246.4 2.8 %convert_multiply_fusion.1 = f32[512,512]{1,0:T(8,128)} fusion(bf16[512,512]{1,0:T(8,128)(2,1)} %get-tuple-element.9, f32[]{:T(128)} %bitcast.3), kind=kLoop, calls=%fused_computation.1 | loop fusion | flops 524288 | bytes 1572868 | tf_op jit(solution)/shard_map/mul | solution.py:964
  (1 shorter events, 0.0 us)
